TPU v7x, 32 devices: a whole 2x2x4 slice. The times are simulated.
32 devices in a mesh: dp: 8 (over y, x, core), tensor: 4 (over z).
Axes of the slice: x: 2, y: 2, z: 4, core: 2. Of those that a mesh axis runs over, the one named last changes fastest.
Arguments:
- tokens: int32 [8, 1024], P('dp', 'tensor'), may hold values from 0 to 50271
- segments: int32 [8, 1024], P('dp'), may hold values from 0 to 12, never falling along the last dimension, each value on 1 to 256 neighbouring positions
- parents: int32 [8, 13], P('dp'), may hold values from 0 to 4, as said below
- completion: int32 [8, 256], P('dp', 'tensor'), may hold values from -1 to 1023, as said below
- targets: int32 [8, 256], P('dp', 'tensor'), may hold values from 0 to 50271
- table: float32 [50272, 512], P('dp')
- table_moment: float32 [50272, 512], P('dp'), may hold values from -0.00390625 to 0.00390625
- vectors: float32 [12, 1024], replicated
- vector_moment: float32 [12, 1024], replicated, may hold values from -0.0234375 to 0.0234375
- w_in: float32 [512, 1024], P('dp'), may hold values from -3 to 3
- moment_in: float32 [512, 1024], P('dp'), may hold values from -0.0234375 to 0.0234375
- error_in: float32 [8, 512, 1024], P('dp'), may hold values from -0.0078125 to 0.0078125
- factor_in: float32 [1024, 8], replicated, may hold values from -6 to 6
- w_qkv: float32 [1024, 3, 1024], P('dp', None, 'tensor'), may hold values from -0.1875 to 0.1875
- moment_qkv: float32 [1024, 3, 1024], P('dp', None, 'tensor'), may hold values from -0.0234375 to 0.0234375
- error_qkv: float32 [8, 1024, 3, 1024], P('dp', None, None, 'tensor'), may hold values from -0.0078125 to 0.0078125
- factor_qkv: float32 [3, 1024, 8], P(None, 'tensor'), may hold values from -6 to 6
- w_proj: float32 [1024, 1024], P('tensor', 'dp'), may hold values from -3.5 to 3.5
- moment_proj: float32 [1024, 1024], P('tensor', 'dp'), may hold values from -0.0234375 to 0.0234375
- error_proj: float32 [8, 1024, 1024], P('dp', 'tensor'), may hold values from -0.0078125 to 0.0078125
- factor_proj: float32 [4, 1024, 8], P('tensor'), may hold values from -6 to 6
- w_up: float32 [1024, 4096], P('dp', 'tensor'), may hold values from -0.1875 to 0.1875
- moment_up: float32 [1024, 4096], P('dp', 'tensor'), may hold values from -0.0234375 to 0.0234375
- error_up: float32 [8, 1024, 4096], P('dp', None, 'tensor'), may hold values from -0.0078125 to 0.0078125
- factor_up: float32 [4096, 8], P('tensor'), may hold values from -6 to 6
- w_down: float32 [4096, 1024], P('tensor', 'dp'), may hold values from -0.09375 to 0.09375
- moment_down: float32 [4096, 1024], P('tensor', 'dp'), may hold values from -0.0234375 to 0.0234375
- error_down: float32 [8, 4096, 1024], P('dp', 'tensor'), may hold values from -0.0078125 to 0.0078125
- factor_down: float32 [4, 1024, 8], P('tensor'), may hold values from -6 to 6
- w_out: float32 [1024, 512], P('dp'), may hold values from -0.1875 to 0.1875
- moment_out: float32 [1024, 512], P('dp'), may hold values from -0.0234375 to 0.0234375
- error_out: float32 [8, 1024, 512], P('dp'), may hold values from -0.0078125 to 0.0078125
- factor_out: float32 [512, 8], replicated, may hold values from -6 to 6
Outputs:
- loss_sum: float32 [], replicated
- new_table: float32 [50272, 512], P('dp')
- new_table_moment: float32 [50272, 512], P('dp')
- new_vectors: float32 [12, 1024], replicated
- new_vector_moment: float32 [12, 1024], replicated
- new_w_in: float32 [512, 1024], P('dp')
- new_moment_in: float32 [512, 1024], P('dp')
- new_error_in: float32 [8, 512, 1024], P('dp')
- new_factor_in: float32 [1024, 8], replicated
- new_w_qkv: float32 [1024, 3, 1024], P('dp', None, 'tensor')
- new_moment_qkv: float32 [1024, 3, 1024], P('dp', None, 'tensor')
- new_error_qkv: float32 [8, 1024, 3, 1024], P('dp', None, None, 'tensor')
- new_factor_qkv: float32 [3, 1024, 8], P(None, 'tensor')
- new_w_proj: float32 [1024, 1024], P('tensor', 'dp')
- new_moment_proj: float32 [1024, 1024], P('tensor', 'dp')
- new_error_proj: float32 [8, 1024, 1024], P('dp', 'tensor')
- new_factor_proj: float32 [4, 1024, 8], P('tensor')
- new_w_up: float32 [1024, 4096], P('dp', 'tensor')
- new_moment_up: float32 [1024, 4096], P('dp', 'tensor')
- new_error_up: float32 [8, 1024, 4096], P('dp', None, 'tensor')
- new_factor_up: float32 [4096, 8], P('tensor')
- new_w_down: float32 [4096, 1024], P('tensor', 'dp')
- new_moment_down: float32 [4096, 1024], P('tensor', 'dp')
- new_error_down: float32 [8, 4096, 1024], P('dp', 'tensor')
- new_factor_down: float32 [4, 1024, 8], P('tensor')
- new_w_out: float32 [1024, 512], P('dp')
- new_moment_out: float32 [1024, 512], P('dp')
- new_error_out: float32 [8, 1024, 512], P('dp')
- new_factor_out: float32 [512, 8], replicated
Inputs may be any that keep to these rules, and one draw needn't show every extreme that they name: `parents`: in every tree segment 0 is the trunk and its own parent, segments 1 to 4 are branches with parent 0, and segments 5 to 12 are leaves, two under each branch. `completion`: each device's 64 slots hold distinct positions of that device's 256 positions of its tree; the live slots come first, slot 0 holds the block's last position, the rest are -1; on the last tree every slot is live.
All inputs are finite; a program needn't handle non-finite values.
Results may differ from a plain program's by a relative error of at most 0.012.
The roundings to bfloat16 on the way count: a program that leaves them out, or rounds other values in their place, can miss the bound.
Values may be sent and summed in bfloat16 or wider, within the bound.
No kernel may reach another device: no remote copies, remote signals or barrier semaphores. Data moves between devices by JAX's collectives and lax.ppermute only.
A program may use at most 320 MiB of HBM per device.

v0:
```python
import jax
import jax.numpy as jnp
from jax import lax
from jax.sharding import PartitionSpec as P

HD = 64


momentum_decay = 0.9
table_rate = 300.0
vector_rate = 1000.0
matrix_rates = (1500.0, 80.0, 3000.0, 80.0, 40.0, 80.0)


def combined_all(part, axis, combine):
    gathered = jax.tree.map(lambda a: lax.all_gather(a, axis), part)

    def take(source):
        return jax.tree.map(lambda a: lax.dynamic_index_in_dim(a, source, 0, False), gathered)

    return lax.fori_loop(
        1, lax.axis_size(axis), lambda source, state: combine(state, take(source)), take(0)
    )


def to_low(values):
    return values.astype(jnp.bfloat16)


def dense(left, right):
    return jnp.dot(left, right, preferred_element_type=jnp.float32)


def dense_first(left, right):
    return lax.dot_general(
        left, right, (((0,), (0,)), ((), ())), preferred_element_type=jnp.float32
    )


def dense_last(left, right):
    return lax.dot_general(
        left, right, (((1,), (1,)), ((), ())), preferred_element_type=jnp.float32
    )


def precise(left, right):
    return jnp.dot(left, right, precision=lax.Precision.HIGHEST)


def precise_first(left, right):
    return lax.dot_general(left, right, (((0,), (0,)), ((), ())), precision=lax.Precision.HIGHEST)


def layer_norm(values, gain, shift):
    center = values - jnp.mean(values, -1, keepdims=True)
    spread = jnp.mean(center * center, -1, keepdims=True)
    return center * lax.rsqrt(spread + 1e-05) * gain + shift


def gelu_tanh(values):
    return jax.nn.gelu(values, approximate=True)


def orthonormal(matrix):
    columns = []
    for index in range(matrix.shape[1]):
        vector = matrix[:, index]
        for previous in columns:
            vector = vector - jnp.sum(previous * vector) * previous
        vector = vector * lax.rsqrt(jnp.sum(vector * vector) + 1e-06)
        columns.append(vector)
    return jnp.stack(columns, 1)


def seq_gather(values):
    return lax.all_gather(values, "tensor", axis=0, tiled=True)


def seq_scatter(values):
    return lax.psum_scatter(values, "tensor", scatter_dimension=0, tiled=True)


def ancestry(segs, parent_row):
    codes = jnp.arange(parent_row.shape[0])
    first = jnp.sum(jnp.where(segs[:, None] == codes[None, :], parent_row[None, :], 0), 1)
    second = jnp.sum(jnp.where(first[:, None] == codes[None, :], parent_row[None, :], 0), 1)
    return (first, second)


def visible_mask(start, block, segs, first, second):
    rows = start + jnp.arange(block)
    columns = jnp.arange(segs.shape[0])
    own = lax.dynamic_slice_in_dim(segs, start, block)
    upper_one = lax.dynamic_slice_in_dim(first, start, block)
    upper_two = lax.dynamic_slice_in_dim(second, start, block)
    related = (
        (segs[None, :] == own[:, None])
        | (segs[None, :] == upper_one[:, None])
        | (segs[None, :] == upper_two[:, None])
    )
    return related & (columns[None, :] <= rows[:, None])


def attend_forward(queries, keys_all, values_all, segs, first, second, block):
    length = queries.shape[0]
    scale = queries.shape[-1] ** (-0.5)

    def one_block(start):
        query_block = lax.dynamic_slice_in_dim(queries, start, block, 0)
        visible = visible_mask(start, block, segs, first, second)
        scores = (
            jnp.einsum("qhe,khe->hqk", query_block, keys_all, preferred_element_type=jnp.float32)
            * scale
        )
        scores = jnp.where(visible[None], scores, -1e30)
        top = jnp.max(scores, -1, keepdims=True)
        expo = jnp.exp(scores - top)
        total = jnp.sum(expo, -1, keepdims=True)
        probs = to_low(expo / total)
        result = jnp.einsum("hqk,khe->qhe", probs, values_all, preferred_element_type=jnp.float32)
        return (result, (top + jnp.log(total))[..., 0])

    results, lse = lax.map(one_block, jnp.arange(0, length, block))
    return (results.reshape(length, -1), lse)


def attend_backward(queries, keys_all, values_all, grad_low, lse, segs, first, second, block):
    length = queries.shape[0]
    scale = queries.shape[-1] ** (-0.5)

    def one_block(carry, pack):
        start, lse_block = pack
        query_block = lax.dynamic_slice_in_dim(queries, start, block, 0)
        grad_block = lax.dynamic_slice_in_dim(grad_low, start, block, 0)
        visible = visible_mask(start, block, segs, first, second)
        scores = (
            jnp.einsum("qhe,khe->hqk", query_block, keys_all, preferred_element_type=jnp.float32)
            * scale
        )
        probs = jnp.where(visible[None], jnp.exp(scores - lse_block[..., None]), 0.0)
        dprobs = jnp.einsum(
            "qhe,khe->hqk", grad_block, values_all, preferred_element_type=jnp.float32
        )
        rowdot = jnp.sum(probs * dprobs, -1, keepdims=True)
        dscores = to_low(probs * (dprobs - rowdot))
        query_grad = (
            jnp.einsum("hqk,khe->qhe", dscores, keys_all, preferred_element_type=jnp.float32)
            * scale
        )
        key_grad = (
            carry[0]
            + jnp.einsum("hqk,qhe->khe", dscores, query_block, preferred_element_type=jnp.float32)
            * scale
        )
        value_grad = carry[1] + jnp.einsum(
            "hqk,qhe->khe", to_low(probs), grad_block, preferred_element_type=jnp.float32
        )
        return ((key_grad, value_grad), query_grad)

    zeros = jnp.zeros(keys_all.shape, jnp.float32)
    (key_grad, value_grad), query_grad = lax.scan(
        one_block, (zeros, zeros), (jnp.arange(0, length, block), lse)
    )
    return (query_grad.reshape(keys_all.shape), key_grad, value_grad)


def combine_stats(left, right):
    top = jnp.maximum(left[0], right[0])
    total = left[1] * jnp.exp(left[0] - top) + right[1] * jnp.exp(right[0] - top)
    return (top, total, left[2] + right[2])


def advance(weight, moment, approx, rate):
    fresh_moment = momentum_decay * moment + approx
    return (weight - rate * fresh_moment, fresh_moment)


def per_device(
    tokens,
    segments,
    parents,
    completion,
    targets,
    table,
    table_moment,
    vectors,
    vector_moment,
    w_in,
    moment_in,
    error_in,
    factor_in,
    w_qkv,
    moment_qkv,
    error_qkv,
    factor_qkv,
    w_proj,
    moment_proj,
    error_proj,
    factor_proj,
    w_up,
    moment_up,
    error_up,
    factor_up,
    w_down,
    moment_down,
    error_down,
    factor_down,
    w_out,
    moment_out,
    error_out,
    factor_out,
):
    dp_count = lax.axis_size("dp")
    tensor_count = lax.axis_size("tensor")
    dp_index = lax.axis_index("dp")
    tensor_index = lax.axis_index("tensor")
    token_ids = tokens[0]
    local_count = token_ids.shape[0]
    segs = segments[0]
    length = segs.shape[0]
    shard_rows = table.shape[0]
    vocab_start = dp_index * shard_rows
    width = w_qkv.shape[2]
    hidden_share = w_up.shape[1]
    model_width = vectors.shape[1]
    heads_here = width // HD
    block = min(512, length)
    full_in, full_qkv, full_proj, full_up, full_down, full_out = (
        lax.all_gather(to_low(w_in), "dp", axis=0, tiled=True),
        lax.all_gather(to_low(w_qkv), "dp", axis=0, tiled=True),
        lax.all_gather(to_low(w_proj), "dp", axis=1, tiled=True),
        lax.all_gather(to_low(w_up), "dp", axis=0, tiled=True),
        lax.all_gather(to_low(w_down), "dp", axis=1, tiled=True),
        lax.all_gather(to_low(w_out), "dp", axis=0, tiled=True),
    )
    comp_row = completion[0]
    target_row = targets[0]
    all_ids, all_comp, all_targets = (
        lax.all_gather(token_ids, "dp", axis=0, tiled=True),
        lax.all_gather(comp_row, "dp", axis=0, tiled=True),
        lax.all_gather(target_row, "dp", axis=0, tiled=True),
    )
    table_low = to_low(table)
    piece = lax.all_gather(table_low, "dp", axis=0, tiled=True)
    wanted = token_ids
    inside = (wanted >= 0) & (wanted < piece.shape[0])
    picked = jnp.take(piece, jnp.clip(wanted, 0, piece.shape[0] - 1), axis=0)
    embedded = jnp.where(inside[:, None], picked.astype(jnp.float32), 0.0)
    emb_low = to_low(embedded)
    x_zero = dense(emb_low, full_in)
    first, second = ancestry(segs, parents[0])
    x_all = seq_gather(to_low(x_zero))
    bias_query = lax.dynamic_slice_in_dim(vectors[4], tensor_index * width, width)
    bias_value = lax.dynamic_slice_in_dim(vectors[5], tensor_index * width, width)
    bias_three = jnp.stack([bias_query, jnp.zeros_like(bias_query), bias_value])
    mixed = (
        jnp.einsum("ld,dch->lch", x_all, full_qkv, preferred_element_type=jnp.float32) + bias_three
    )
    mixed_low = to_low(mixed).reshape(length, 3, heads_here, HD)
    queries = mixed_low[:, 0]
    keys_all = mixed_low[:, 1]
    values_all = mixed_low[:, 2]
    attended, lse = attend_forward(queries, keys_all, values_all, segs, first, second, block)
    attn_low = to_low(attended)
    z_branch = seq_scatter(dense(attn_low, full_proj))
    pre_one = x_zero + z_branch + vectors[6]
    h_one = layer_norm(pre_one, vectors[0], vectors[1])
    h_all = seq_gather(to_low(h_one))
    bias_up = lax.dynamic_slice_in_dim(
        vectors[8:].reshape(-1), tensor_index * hidden_share, hidden_share
    )
    upper = dense(h_all, full_up) + bias_up
    act_low = to_low(gelu_tanh(upper))
    f_branch = seq_scatter(dense(act_low, full_down))
    pre_two = h_one + f_branch + vectors[7]
    h_two = layer_norm(pre_two, vectors[2], vectors[3])
    h_two_low = to_low(h_two)
    output = dense(h_two_low, full_out)
    local_spot = jnp.clip(comp_row - tensor_index * local_count, 0, local_count - 1)
    rows_low = to_low(jnp.take(output, local_spot, axis=0))
    all_rows = lax.all_gather(rows_low, "dp", axis=0, tiled=True)
    total_rows = all_rows.shape[0]
    head_block = min(512, total_rows)
    head_count = total_rows // head_block
    vocab_ids = vocab_start + jnp.arange(shard_rows)
    row_blocks = all_rows.reshape(head_count, head_block, -1)
    target_blocks = all_targets.reshape(head_count, head_block)

    def head_stats(pack):
        rows_block, target_block = pack
        logits = dense_last(rows_block, table_low)
        top = jnp.max(logits, -1)
        total = jnp.sum(jnp.exp(logits - top[:, None]), -1)
        picked = jnp.sum(jnp.where(vocab_ids[None, :] == target_block[:, None], logits, 0.0), -1)
        return (top, total, picked)

    stats = lax.map(head_stats, (row_blocks, target_blocks))
    top, total, picked = combined_all(
        (stats[0].reshape(-1), stats[1].reshape(-1), stats[2].reshape(-1)), "dp", combine_stats
    )
    lse_rows = top + jnp.log(total)
    valid_rows = all_comp >= 0
    loss_part = jnp.sum(jnp.where(valid_rows, lse_rows - picked, 0.0))
    row_weight = jnp.where(valid_rows, 1.0, 0.0) * (
        1.0 / (dp_count * tensor_count * comp_row.shape[0])
    )

    def head_back(carry, pack):
        rows_block, target_block, lse_block, weight_block = (pack[0], pack[1], pack[2], pack[3])
        logits = dense_last(rows_block, table_low)
        onehot = jnp.where(vocab_ids[None, :] == target_block[:, None], 1.0, 0.0)
        grad_low = to_low((jnp.exp(logits - lse_block[:, None]) - onehot) * weight_block[:, None])
        return (carry + dense_first(grad_low, rows_block), dense(grad_low, table_low))

    packs = (
        row_blocks,
        target_blocks,
        lse_rows.reshape(head_count, head_block),
        row_weight.reshape(head_count, head_block),
    ) + ()
    table_grad, row_grads = lax.scan(head_back, jnp.zeros(table.shape, jnp.float32), packs)
    out_rows = lax.psum_scatter(
        row_grads.reshape(total_rows, -1), "dp", scatter_dimension=0, tiled=True
    )
    output_grad = (
        jnp.zeros(output.shape, jnp.float32)
        .at[local_spot]
        .add(jnp.where((comp_row >= 0)[:, None], out_rows, 0.0))
    )
    out_low = to_low(output_grad)
    grad_out = dense_first(h_two_low, out_low)
    h_two_grad = dense_last(out_low, full_out)
    norm_two = jax.vjp(layer_norm, pre_two, vectors[2], vectors[3])[1]
    pre_two_grad, gain_two_grad, shift_two_grad = norm_two(h_two_grad)
    f_all = seq_gather(to_low(pre_two_grad))
    grad_down = dense_first(act_low, f_all)
    act_grad = dense_last(f_all, full_down)
    upper_grad = jax.vjp(gelu_tanh, upper)[1](act_grad)[0]
    upper_low = to_low(upper_grad)
    grad_up = dense_first(h_all, upper_low)
    h_one_grad = pre_two_grad + seq_scatter(dense_last(upper_low, full_up))
    norm_one = jax.vjp(layer_norm, pre_one, vectors[0], vectors[1])[1]
    pre_one_grad, gain_one_grad, shift_one_grad = norm_one(h_one_grad)
    z_all = seq_gather(to_low(pre_one_grad))
    grad_proj = dense_first(attn_low, z_all)
    attn_grad = to_low(dense_last(z_all, full_proj)).reshape(length, heads_here, HD)
    query_grad, key_grad, value_grad = attend_backward(
        queries, keys_all, values_all, attn_grad, lse, segs, first, second, block
    )
    mixed_grad = to_low(jnp.stack([query_grad, key_grad, value_grad], 1).reshape(length, 3, width))
    grad_qkv = jnp.einsum("ld,lch->dch", x_all, mixed_grad, preferred_element_type=jnp.float32)
    x_grad = pre_one_grad + seq_scatter(
        jnp.einsum("lch,dch->ld", mixed_grad, full_qkv, preferred_element_type=jnp.float32)
    )
    x_grad_low = to_low(x_grad)
    grad_in = dense_first(emb_low, x_grad_low)
    emb_grad = to_low(dense_last(x_grad_low, full_in))
    wanted = all_ids - vocab_start
    inside = (wanted >= 0) & (wanted < shard_rows)
    values = jnp.where(
        inside[:, None], lax.all_gather(emb_grad, "dp", axis=0, tiled=True).astype(jnp.float32), 0.0
    )
    table_grad = table_grad + jax.ops.segment_sum(
        values, jnp.clip(wanted, 0, shard_rows - 1), num_segments=shard_rows
    )

    def placed(values, size, total_size):
        return lax.dynamic_update_slice_in_dim(
            jnp.zeros((total_size,), jnp.float32), values, tensor_index * size, 0
        )

    mixed_sums = jnp.sum(mixed_grad.astype(jnp.float32), 0)
    head_rows = jnp.stack(
        [
            gain_one_grad,
            shift_one_grad,
            gain_two_grad,
            shift_two_grad,
            placed(mixed_sums[0], width, model_width),
            placed(mixed_sums[2], width, model_width),
            jnp.sum(pre_one_grad, 0),
            jnp.sum(pre_two_grad, 0),
        ]
    )
    up_rows = placed(
        jnp.sum(upper_low.astype(jnp.float32), 0), hidden_share, hidden_share * tensor_count
    ).reshape(-1, model_width)
    vector_part = jnp.concatenate([head_rows, up_rows], 0)
    grad_table, grad_in_sum, grad_out_sum, vector_tensor, loss_sum = lax.psum(
        (table_grad, grad_in, grad_out, vector_part, loss_part), "tensor"
    )
    merged = (
        grad_in_sum + error_in[0],
        grad_qkv.reshape(model_width, 3 * width) + error_qkv[0].reshape(model_width, 3 * width),
        grad_proj + error_proj[0],
        grad_up + error_up[0],
        grad_down + error_down[0],
        grad_out_sum + error_out[0],
    )
    factors = (
        factor_in,
        factor_qkv.reshape(3 * width, -1),
        factor_proj[0],
        factor_up,
        factor_down[0],
        factor_out,
    )
    summed = lax.psum(
        (
            precise(merged[0], factors[0]),
            precise(merged[1], factors[1]),
            precise(merged[2], factors[2]),
            precise(merged[3], factors[3]),
            precise(merged[4], factors[4]),
            precise(merged[5], factors[5]),
            vector_tensor,
        ),
        "dp",
    )
    bases = [orthonormal(matrix) for matrix in summed[:6]]
    fresh = lax.psum(
        (
            precise_first(merged[0], bases[0]),
            precise_first(merged[1], bases[1]),
            precise_first(merged[2], bases[2]),
            precise_first(merged[3], bases[3]),
            precise_first(merged[4], bases[4]),
            precise_first(merged[5], bases[5]),
        ),
        "dp",
    )
    approx = [precise(bases[index], fresh[index].T) for index in range(6)]
    errors_new = [merged[index] - approx[index] / dp_count for index in range(6)]
    shard_in = lax.dynamic_slice_in_dim(approx[0], dp_index * w_in.shape[0], w_in.shape[0], 0)
    shard_qkv = lax.dynamic_slice_in_dim(
        approx[1].reshape(model_width, 3, width), dp_index * w_qkv.shape[0], w_qkv.shape[0], 0
    )
    shard_proj = lax.dynamic_slice_in_dim(approx[2], dp_index * w_proj.shape[1], w_proj.shape[1], 1)
    shard_up = lax.dynamic_slice_in_dim(approx[3], dp_index * w_up.shape[0], w_up.shape[0], 0)
    shard_down = lax.dynamic_slice_in_dim(approx[4], dp_index * w_down.shape[1], w_down.shape[1], 1)
    shard_out = lax.dynamic_slice_in_dim(approx[5], dp_index * w_out.shape[0], w_out.shape[0], 0)
    new_w_in, new_moment_in = advance(w_in, moment_in, shard_in, matrix_rates[0])
    new_w_qkv, new_moment_qkv = advance(w_qkv, moment_qkv, shard_qkv, matrix_rates[1])
    new_w_proj, new_moment_proj = advance(w_proj, moment_proj, shard_proj, matrix_rates[2])
    new_w_up, new_moment_up = advance(w_up, moment_up, shard_up, matrix_rates[3])
    new_w_down, new_moment_down = advance(w_down, moment_down, shard_down, matrix_rates[4])
    new_w_out, new_moment_out = advance(w_out, moment_out, shard_out, matrix_rates[5])
    new_table, new_table_moment = advance(table, table_moment, grad_table, table_rate)
    new_vectors, new_vector_moment = advance(vectors, vector_moment, summed[6], vector_rate)
    return (
        loss_sum,
        new_table,
        new_table_moment,
        new_vectors,
        new_vector_moment,
        new_w_in,
        new_moment_in,
        errors_new[0][None],
        fresh[0],
        new_w_qkv,
        new_moment_qkv,
        errors_new[1].reshape(1, model_width, 3, width),
        fresh[1].reshape(3, width, -1),
        new_w_proj,
        new_moment_proj,
        errors_new[2][None],
        fresh[2][None],
        new_w_up,
        new_moment_up,
        errors_new[3][None],
        fresh[3],
        new_w_down,
        new_moment_down,
        errors_new[4][None],
        fresh[4][None],
        new_w_out,
        new_moment_out,
        errors_new[5][None],
        fresh[5],
    )


def solution(mesh):
    return jax.shard_map(
        per_device,
        mesh=mesh,
        in_specs=(
            P("dp", "tensor"),
            P("dp", None),
            P("dp", None),
            P("dp", "tensor"),
            P("dp", "tensor"),
            P("dp", None),
            P("dp", None),
            P(),
            P(),
            P("dp", None),
            P("dp", None),
            P("dp", None, None),
            P(),
            P("dp", None, "tensor"),
            P("dp", None, "tensor"),
            P("dp", None, None, "tensor"),
            P(None, "tensor", None),
            P("tensor", "dp"),
            P("tensor", "dp"),
            P("dp", "tensor", None),
            P("tensor", None, None),
            P("dp", "tensor"),
            P("dp", "tensor"),
            P("dp", None, "tensor"),
            P("tensor", None),
            P("tensor", "dp"),
            P("tensor", "dp"),
            P("dp", "tensor", None),
            P("tensor", None, None),
            P("dp", None),
            P("dp", None),
            P("dp", None, None),
            P(),
        ),
        out_specs=(
            P(),
            P("dp", None),
            P("dp", None),
            P(),
            P(),
            P("dp", None),
            P("dp", None),
            P("dp", None, None),
            P(),
            P("dp", None, "tensor"),
            P("dp", None, "tensor"),
            P("dp", None, None, "tensor"),
            P(None, "tensor", None),
            P("tensor", "dp"),
            P("tensor", "dp"),
            P("dp", "tensor", None),
            P("tensor", None, None),
            P("dp", "tensor"),
            P("dp", "tensor"),
            P("dp", None, "tensor"),
            P("tensor", None),
            P("tensor", "dp"),
            P("tensor", "dp"),
            P("dp", "tensor", None),
            P("tensor", None, None),
            P("dp", None),
            P("dp", None),
            P("dp", None, None),
            P(),
        ),
        check_vma=False,
    )
```

profile of v0, /device:TPU:0, one launch (start us, length us, event | category | flops | bytes accessed | tf_op | source)
XLA Modules:
  0.0 2321.6 jit_solution(1452442727284911027)
XLA Ops:
  18.2 237.3 %all-gather.42.cloned.1.call-done = bf16[8,6284,512]{2,1,0:T(8,128)(2,1)} async-done(((bf16[1,6284,512]{2,1,0:T(8,128)(2,1)}), bf16[8,6284,512]{2,1,0:T(8,128)(2,1)}) %all-gather.42.cloned.1.call-update) | async-done | bytes 51478544 | tf_op jit(solution)/shard_map/all_gather | solution.py:244
  255.5 47.3 %reshape.635 = bf16[50272,512]{1,0:T(8,128)(2,1)} reshape(bf16[8,6284,512]{2,1,0:T(8,128)(2,1)} %all-gather.42.cloned.1.call-done) | data formatting | bytes 102957056
  309.0 10.2 all_gather.62
  319.2 38.6 %all-gather.24.cloned.1.call-done = bf16[1024,1024]{1,0:T(8,128)(2,1)} async-done(((bf16[256,1024]{1,0:T(8,128)(2,1)}), bf16[1024,1024]{1,0:T(8,128)(2,1)}) %all-gather.24.cloned.1.call-update) | async-done | bytes 2097168 | tf_op jit(solution)/shard_map/all_gather | solution.py:76
  361.9 23.3 %while.16 = (s32[]{:T(128)}, bf16[2,512,4,64]{1,3,2,0:T(8,128)(2,1)S(1)}, f32[2,4,512]{2,1,0:T(4,128)S(1)}, s32[1,1024]{1,0:T(1,128)S(1)}, s32[2]{0:T(128)S(1)},...) while((s32[]{:T(128)}, ...), condition=%wide.region_5.6_spmd, body=%wide.region_2.5_spmd.sunk | while | flops 565705216 | bytes 29190352 | solution.py:123
  390.4 73.8 %reduce-scatter.6.cloned.1.call-done = f32[256,1024]{1,0:T(8,128)} async-done(((f32[1024,1024]{1,0:T(8,128)}), f32[256,1024]{1,0:T(8,128)}) %reduce-scatter.6.cloned.1.call-update) | async-done | bytes 1048592 | tf_op jit(solution)/shard_map/reduce_scatter | solution.py:80
  468.6 26.5 %all-gather.30.cloned.1.call-done = bf16[1024,1024]{1,0:T(8,128)(2,1)} async-done(((bf16[128,1024]{1,0:T(8,128)(2,1)}), bf16[1024,1024]{1,0:T(8,128)(2,1)}) %all-gather.30.cloned.1.call-update) | async-done | bytes 2097168 | tf_op jit(solution)/shard_map/all_gather | solution.py:232
  495.2 48.2 %all-gather.28.cloned.1.call-done = bf16[1024,1024]{1,0:T(8,128)(2,1)} async-done(((bf16[256,1024]{1,0:T(8,128)(2,1)}), bf16[1024,1024]{1,0:T(8,128)(2,1)}) %all-gather.28.cloned.1.call-update) | async-done | bytes 2097168 | tf_op jit(solution)/shard_map/all_gather | solution.py:76
  549.9 23.0 all-gather.32.cloned.1.call-done
  590.8 66.7 %reduce-scatter.8.cloned.1.call-done = f32[256,1024]{1,0:T(8,128)} async-done(((f32[1024,1024]{1,0:T(8,128)}), f32[256,1024]{1,0:T(8,128)}) %reduce-scatter.8.cloned.1.call-update) | async-done | bytes 1048592 | tf_op jit(solution)/shard_map/reduce_scatter | solution.py:80
  660.4 23.5 %all-gather.34.cloned.1.call-done = bf16[1024,512]{1,0:T(8,128)(2,1)} async-done(((bf16[128,512]{1,0:T(8,128)(2,1)}), bf16[1024,512]{1,0:T(8,128)(2,1)}) %all-gather.34.cloned.1.call-update) | async-done | bytes 1048592 | tf_op jit(solution)/shard_map/all_gather | solution.py:234
  686.7 9.8 all_gather.67
  752.1 36.1 %reduce-scatter.10.cloned.1.call-done = f32[64,512]{1,0:T(8,128)} async-done(((f32[512,512]{1,0:T(8,128)}), f32[64,512]{1,0:T(8,128)}) %reduce-scatter.10.cloned.1.call-update) | async-done | bytes 131088 | tf_op jit(solution)/shard_map/reduce_scatter | solution.py:322
  797.1 46.0 %all-gather.36.cloned.1.call-done = bf16[1024,1024]{1,0:T(8,128)(2,1)} async-done(((bf16[256,1024]{1,0:T(8,128)(2,1)}), bf16[1024,1024]{1,0:T(8,128)(2,1)}) %all-gather.36.cloned.1.call-update) | async-done | bytes 2097168 | tf_op jit(solution)/shard_map/all_gather | solution.py:76
  857.3 75.6 %reduce-scatter.12.cloned.1.call-done = f32[256,1024]{1,0:T(8,128)} async-done(((f32[1024,1024]{1,0:T(8,128)}), f32[256,1024]{1,0:T(8,128)}) %reduce-scatter.12.cloned.1.call-update) | async-done | bytes 1048592 | tf_op jit(solution)/shard_map/reduce_scatter | solution.py:80
  938.0 46.5 %all-gather.38.cloned.1.call-done = bf16[1024,1024]{1,0:T(8,128)(2,1)} async-done(((bf16[256,1024]{1,0:T(8,128)(2,1)}), bf16[1024,1024]{1,0:T(8,128)(2,1)}) %all-gather.38.cloned.1.call-update) | async-done | bytes 2097168 | tf_op jit(solution)/shard_map/all_gather | solution.py:76
  988.5 49.8 %while.59 = (s32[]{:T(128)}, f32[1024,4,64]{0,2,1:T(8,128)S(1)}, f32[1024,4,64]{0,2,1:T(8,128)}, bf16[2,512,4,64]{1,3,2,0:T(8,128)(2,1)}, s32[2]{0:T(128)S(1)}, ...) while((s32[]{:T(128)}, f32[1024,4,64]{0,2,1:T(8,128)S(1)}, ...), condition=%wide.region_28.29_spmd.clone, body=%wide.region_26.28_spmd.clone.sunk | while | flops 1378744832 | bytes 143739760 | solution.py:161
  1050.9 75.2 %reduce-scatter.14.cloned.1.call-done = f32[256,1024]{1,0:T(8,128)} async-done(((f32[1024,1024]{1,0:T(8,128)}), f32[256,1024]{1,0:T(8,128)}) %reduce-scatter.14.cloned.1.call-update) | async-done | bytes 1048592 | tf_op jit(solution)/shard_map/reduce_scatter | solution.py:80
  1130.0 8.9 all-gather.5
  1139.0 11.4 fusion.104
  1158.5 24.1 %scatter_custom_fusion.1 = f32[6284,512]{1,0:T(8,128)} fusion(f32[6284,512]{1,0:T(8,128)} %fusion.104, s32[2048]{0:T(1024)S(1)} %bitcast.522, bf16[2048,512]{1,0:T(8,128)(2,1)} %all-gather.40.cloned.1.call-done, f32[]{:T(128)} %constant.236.clone.1, pred[2048]{0:T(1024)(128)(4,1)S(1)} %and_reduce_fusion), kind=kCustom, calls=%fused_computation.78 | custom fusion | flops 3145728 | bytes 14969344 | tf_op jit(solution)/shard_map/scatter-add | solution.py:363
  1222.4 534.2 %all-reduce.15.cloned.1.call-done = (f32[6284,512]{1,0:T(8,128)}, f32[512,1024]{1,0:T(8,128)}, f32[1024,512]{1,0:T(8,128)}) async-done(((f32[6284,512]{1,0:T(8,128)}, f32[512,1024]{1,0:T(8,128)}, f32[1024,512]{1,0:T(8,128)}), (f32[6284,512]{1,0:T(8,128)}, f32[512,1024]{1,0:T(8,128)}, f32[1024,512]{1,0:T(8,128)})) %all-reduce.15.cloned.1.call-update) | async-done | bytes 17063952 | tf_op jit(solution)/shard_map/psum | solution.py:389
  1764.3 18.6 all-reduce.5
  1782.9 34.0 %all-reduce.13.cloned.1.call-done = (f32[512,8]{0,1:T(8,128)}, f32[1024,8]{0,1:T(8,128)}, f32[256,8]{0,1:T(8,128)}, f32[1024,8]{0,1:T(8,128)}, f32[1024,8]{0,1:T(8,128)}, /*index=5*/f32[1024,8]{0,1:T(8,128)}) async-done(((f32[512,8]{0,1:T(8,128)}, f32[1024,8]{0,1:T(8,128)}, f32[256,8]{0,1:T(8,128)}, f32[1024,8]{0,1:T(8,128)}, f32[1024,8]{0,1:T(8,128)}, /*index=5*/f32[1024,8]{0,1:T(8,128)}), ...) | async-done | bytes 155664 | tf_op jit(solution)/shard_map/psum | solution.py:408
  1861.8 19.2 subtract_multiply_fusion
  1928.4 18.2 subtract_multiply_fusion.7
  1994.8 18.1 subtract_multiply_fusion.14
  2061.0 18.1 subtract_multiply_fusion.35
  2124.7 18.0 subtract_multiply_fusion.21
  2190.2 17.9 subtract_multiply_fusion.28
  2212.3 23.4 %multiply_subtract_fusion = (f32[6284,512]{1,0:T(8,128)}, f32[6284,512]{1,0:T(8,128)}) fusion(f32[6284,512]{1,0:T(8,128)} %param.44, f32[6284,512]{1,0:T(8,128)} %get-tuple-element.810, f32[6284,512]{1,0:T(8,128)} %param.45), kind=kLoop, calls=%fused_computation.61 | loop fusion | flops 12869632 | bytes 64348160 | tf_op jit(solution)/shard_map/sub | solution.py:175
  2235.6 31.7 %all-reduce.11.cloned.1.call-done = (f32[12,1024]{1,0:T(8,128)}, f32[1024,8]{0,1:T(8,128)}, f32[768,8]{0,1:T(8,128)}, f32[1024,8]{0,1:T(8,128)}, f32[1024,8]{0,1...) async-done(((f32[12,1024]{1,0:T(8,128)}, f32[1024,8]{0,1:T(8,128)}, f32[768,8]{0,1:T(8,128)}, f32[1024,8]{0,1:T(8,128)}, f32[1024,8]{0,1:T(8,128)}, ...) | async-done | bytes 221200 | tf_op jit(solution)/shard_map/psum | solution.py:408
  (576 shorter events, 584.5 us)
Async XLA Ops:
  7.2 1189.4 %copy-start = (f32[1,1024,8]{1,2,0:T(8,128)S(1)}, f32[1,1024,8]{1,2,0:T(8,128)}, u32[]{:S(2)}) copy-start(f32[1,1024,8]{1,2,0:T(8,128)} %param.67) | copy-start | bytes 98308
  7.2 248.3 %all-gather.42.cloned.1.call-start = ((), (), s32[]{:S(2)}) async-start(), calls=%async_computation.20 | async-start | bytes 57950208 | tf_op jit(solution)/shard_map/all_gather | solution.py:244
  15.5 290.0 %all-gather.22.cloned.1.call-start = ((), (), s32[]{:S(2)}) async-start(), calls=%async_computation.5 | async-start | bytes 1179648 | tf_op jit(solution)/shard_map/all_gather | solution.py:229
  17.1 302.1 %all-gather.26.cloned.1.call-start = ((), (), s32[]{:S(2)}) async-start(), calls=%async_computation.7 | async-start | bytes 1769472 | tf_op jit(solution)/shard_map/all_gather | solution.py:230
  18.0 339.8 %all-gather.24.cloned.1.call-start = ((), (), s32[]{:S(2)}) async-start(), calls=%async_computation.6 | async-start | bytes 2621440 | tf_op jit(solution)/shard_map/all_gather | solution.py:76
  18.2 287.4 %copy-start.83 = (pred[256]{0:T(512)(128)(4,1)}, pred[256]{0:T(512)(128)(4,1)S(1)}, u32[]{:S(2)}) copy-start(pred[256]{0:T(512)(128)(4,1)S(1)} %and_reduce_fusion.1) | copy-start | bytes 772
  18.2 287.4 %copy-start.85 = (pred[256]{0:T(512)(128)(4,1)}, pred[256]{0:T(512)(128)(4,1)S(1)}, u32[]{:S(2)}) copy-start(pred[256]{0:T(512)(128)(4,1)S(1)} %compare_and_fusion) | copy-start | bytes 772
  308.5 155.7 %reduce-scatter.6.cloned.1.call-start = ((), (), s32[]{:S(2)}) async-start(), calls=%async_computation.8 | async-start | bytes 5242880 | tf_op jit(solution)/shard_map/reduce_scatter | solution.py:80
  308.7 375.1 %copy-start.73 = (f32[1,1024]{1,0:T(1,128)}, f32[1,1024]{1,0:T(1,128)S(1)}, u32[]{:S(2)}) copy-start(f32[1,1024]{1,0:T(1,128)S(1)} %get-tuple-element.1032) | copy-start | bytes 12292
  388.6 78.8 %copy-start.33 = (f32[1024,128]{1,0:T(8,128)S(1)}, f32[1024,128]{1,0:T(8,128)}, u32[]{:S(2)}) copy-start(f32[1024,128]{1,0:T(8,128)} %param.64) | copy-start | bytes 1572868
  388.6 106.5 %all-gather.30.cloned.1.call-start = ((), (), s32[]{:S(2)}) async-start(), calls=%async_computation.10 | async-start | bytes 2359296 | tf_op jit(solution)/shard_map/all_gather | solution.py:232
  390.4 152.9 %all-gather.28.cloned.1.call-start = ((), (), s32[]{:S(2)}) async-start(), calls=%async_computation.9 | async-start | bytes 2621440 | tf_op jit(solution)/shard_map/all_gather | solution.py:76
  467.3 105.6 %all-gather.32.cloned.1.call-start = ((), (), s32[]{:S(2)}) async-start(), calls=%async_computation.11 | async-start | bytes 2359296 | tf_op jit(solution)/shard_map/all_gather | solution.py:233
  468.1 189.4 %reduce-scatter.8.cloned.1.call-start = ((), (), s32[]{:S(2)}) async-start(), calls=%async_computation.12 | async-start | bytes 5242880 | tf_op jit(solution)/shard_map/reduce_scatter | solution.py:80
  580.6 103.3 %all-gather.34.cloned.1.call-start = ((), (), s32[]{:S(2)}) async-start(), calls=%async_computation.13 | async-start | bytes 1179648 | tf_op jit(solution)/shard_map/all_gather | solution.py:234
  582.2 206.0 %reduce-scatter.10.cloned.1.call-start = ((), (), s32[]{:S(2)}) async-start(), calls=%async_computation.14 | async-start | bytes 1179648 | tf_op jit(solution)/shard_map/reduce_scatter | solution.py:322
  752.0 91.0 %all-gather.36.cloned.1.call-start = ((), (), s32[]{:S(2)}) async-start(), calls=%async_computation.15 | async-start | bytes 2621440 | tf_op jit(solution)/shard_map/all_gather | solution.py:76
  797.0 135.8 %reduce-scatter.12.cloned.1.call-start = ((), (), s32[]{:S(2)}) async-start(), calls=%async_computation.16 | async-start | bytes 5242880 | tf_op jit(solution)/shard_map/reduce_scatter | solution.py:80
  857.2 127.3 %copy-start.32 = (bf16[256,1024]{1,0:T(8,128)(2,1)S(1)}, bf16[256,1024]{1,0:T(8,128)(2,1)}, u32[]{:S(2)}) copy-start(bf16[256,1024]{1,0:T(8,128)(2,1)} %copy-done.31) | copy-start | bytes 1572868
  857.2 127.2 %all-gather.38.cloned.1.call-start = ((), (), s32[]{:S(2)}) async-start(), calls=%async_computation.17 | async-start | bytes 2621440 | tf_op jit(solution)/shard_map/all_gather | solution.py:76
  937.9 188.2 %reduce-scatter.14.cloned.1.call-start = ((), (), s32[]{:S(2)}) async-start(), calls=%async_computation.18 | async-start | bytes 5242880 | tf_op jit(solution)/shard_map/reduce_scatter | solution.py:80
  1050.5 75.7 %copy-start.17 = (f32[256,1024]{1,0:T(8,128)S(1)}, f32[256,1024]{1,0:T(8,128)}, u32[]{:S(2)}) copy-start(f32[256,1024]{1,0:T(8,128)} %copy-done.16) | copy-start | bytes 3145732
  1050.5 79.6 %copy-start.81 = (s32[1,256]{1,0:T(1,128)S(1)}, s32[1,256]{1,0:T(1,128)}, u32[]{:S(2)}) copy-start(s32[1,256]{1,0:T(1,128)} %param.39) | copy-start | bytes 3076
  1050.5 108.0 %all-gather.40.cloned.1.call-start = ((), (), s32[]{:S(2)}) async-start(), calls=%async_computation.19 | async-start | bytes 2359296 | tf_op jit(solution)/shard_map/all_gather | solution.py:361
  1130.0 626.6 %all-reduce.15.cloned.1.call-start = ((), (), s32[]{:S(2)}) async-start(), calls=%async_computation.23 | async-start | bytes 34144256 | tf_op jit(solution)/shard_map/psum | solution.py:389
  1182.7 634.2 %all-reduce.13.cloned.1.call-start = ((), (), s32[]{:S(2)}) async-start(), calls=%async_computation.22 | async-start | bytes 311296 | tf_op jit(solution)/shard_map/psum | solution.py:408
  1218.2 538.4 %copy-start.72 = (f32[512,8]{0,1:T(8,128)S(1)}, f32[512,8]{0,1:T(8,128)}, u32[]{:S(2)}) copy-start(f32[512,8]{0,1:T(8,128)} %param.71) | copy-start | bytes 49156
  1220.0 541.6 %copy-start.68 = (f32[1024,8]{0,1:T(8,128)S(1)}, f32[1024,8]{0,1:T(8,128)}, u32[]{:S(2)}) copy-start(f32[1024,8]{0,1:T(8,128)} %param.51) | copy-start | bytes 98308
  1764.1 503.2 %all-reduce.11.cloned.1.call-start = ((), (), s32[]{:S(2)}) async-start(), calls=%async_computation.21 | async-start | bytes 475136 | tf_op jit(solution)/shard_map/psum | solution.py:408
  1946.6 71.4 %copy-start.70 = (f32[256,8]{0,1:T(8,128)S(1)}, f32[256,8]{0,1:T(8,128)}, u32[]{:S(2)}) copy-start(f32[256,8]{0,1:T(8,128)} %get-tuple-element.804) | copy-start | bytes 24580
  1951.7 129.9 %copy-start.58 = (f32[1024,8]{0,1:T(8,128)S(1)}, f32[1024,8]{0,1:T(8,128)}, u32[]{:S(2)}) copy-start(f32[1024,8]{0,1:T(8,128)} %get-tuple-element.803) | copy-start | bytes 98308
  2013.0 133.3 %copy-start.66 = (f32[512,8]{0,1:T(8,128)S(1)}, f32[512,8]{0,1:T(8,128)}, u32[]{:S(2)}) copy-start(f32[512,8]{0,1:T(8,128)} %get-tuple-element.802) | copy-start | bytes 49156
  (88 other events, 688.6 us)
Sparse Core Ops, SparseCore 0:
  15.7 239.8 all-gather.41
  258.0 23.4 all-gather.21
  284.0 25.8 all-gather.25
  311.9 45.9 all-gather.23
  388.7 75.4 reduce-scatter.5
  466.7 28.3 all-gather.29
  497.4 45.9 all-gather.27
  545.9 26.9 all-gather.31
  580.7 76.7 reduce-scatter.7
  659.8 24.0 all-gather.33
  752.2 36.0 reduce-scatter.9
  797.1 45.8 all-gather.35
  857.4 75.4 reduce-scatter.11
  938.0 46.4 all-gather.37
  1050.6 75.4 reduce-scatter.13
  1130.1 28.3 all-gather.39
  1182.8 573.7 all-reduce.14
  1764.3 52.5 all-reduce.12
  2212.4 54.8 all-reduce.10
where the time goes:
time: 2330 us; the launch traced here: 2320 us
  waiting for transfers between devices  1420 us (61%)
  other arithmetic  466 us (20%)
  matrix products  203 us (9%)
  local copies, waits for them, and re-layouts  92.7 us (4%)
  blocking collectives  79.3 us (3%)
  between operations  49.3 us (2%)
    psum x1, waiting for transfers between devices, per_device(): lax.psum((table_grad, grad_in, grad_out, vector_part, loss_part), 'tensor')  534 us
    reduce_scatter x4, waiting for transfers between devices, seq_scatter(): return lax.psum_scatter(values, 'tensor', scatter_dimension=0, tiled=True)  291 us
    all_gather x1, waiting for transfers between devices, per_device(): piece = lax.all_gather(table_low, 'dp', axis=0, tiled=True)  237 us
    all_gather x4, waiting for transfers between devices, seq_gather(): return lax.all_gather(values, 'tensor', axis=0, tiled=True)  179 us
    reduce_sum x56, other arithmetic, orthonormal(): vector = vector - jnp.sum(previous * vector) * previous  173 us
    mul x6, other arithmetic, orthonormal(): vector = vector * lax.rsqrt(jnp.sum(vector * vector) + 1e-06)  109 us
    unnamed x208, local copies, waits for them, and re-layouts  75.8 us
    psum x2, waiting for transfers between devices, per_device(): lax.psum((precise(merged[0], factors[0]), precise(merged[1], factors[1]),...  65.6 us
  transfers between devices with their start and end apart: 19, of which 17 were waited for; matrix products, arithmetic and copies ran while one was open for 6% of the time, Pallas kernels for 0%

commit v1 on v0

v1 whole, which is shorter than its diff:
```python
import functools

import jax
import jax.numpy as jnp
from jax import lax
from jax.experimental import pallas as pl
from jax.experimental.pallas import tpu as pltpu
from jax.sharding import PartitionSpec as P

HD = 64


momentum_decay = 0.9
table_rate = 300.0
vector_rate = 1000.0
matrix_rates = (1500.0, 80.0, 3000.0, 80.0, 40.0, 80.0)


def to_low(values):
    return values.astype(jnp.bfloat16)


def dense(left, right):
    return jnp.dot(left, right, preferred_element_type=jnp.float32)


def dense_first(left, right):
    return lax.dot_general(
        left, right, (((0,), (0,)), ((), ())), preferred_element_type=jnp.float32
    )


def dense_last(left, right):
    return lax.dot_general(
        left, right, (((1,), (1,)), ((), ())), preferred_element_type=jnp.float32
    )


left_terms = (0, 0, 1, 1, 0, 2)
right_terms = (0, 1, 0, 1, 2, 0)


def left_factor(merged, factor):
    return lax.dot_general(factor, merged, (((0,), (1,)), ((), ())), precision=lax.Precision.HIGH)


def right_factor(merged, basis):
    return lax.dot_general(basis, merged, (((1,), (0,)), ((), ())), precision=lax.Precision.HIGH)


def layer_norm(values, gain, shift):
    center = values - jnp.mean(values, -1, keepdims=True)
    spread = jnp.mean(center * center, -1, keepdims=True)
    return center * lax.rsqrt(spread + 1e-05) * gain + shift


def gelu_tanh(values):
    return jax.nn.gelu(values, approximate=True)


def swap(values, axis, step):
    return lax.ppermute(values, axis, [(i, i ^ step) for i in range(lax.axis_size(axis))])


def gather_blocks(values, axis):
    return [values] + [swap(values, axis, s) for s in range(1, lax.axis_size(axis))]


def exchange_blocks(blocks, axis):
    return [blocks[0]] + [swap(blocks[s], axis, s) for s in range(1, lax.axis_size(axis))]


def summed_over(values, axis):
    step = 1
    while step < lax.axis_size(axis):
        values = jax.tree.map(lambda a, s=step: a + swap(a, axis, s), values)
        step *= 2
    return values


def add_up(parts):
    total = parts[0].astype(jnp.float32)
    for part in parts[1:]:
        total = total + part.astype(jnp.float32)
    return total


def add_pairs(parts):
    while len(parts) > 1:
        parts = [left + right for left, right in zip(parts[::2], parts[1::2])]
    return parts[0]


def orthonormal_kernel(columns_ref, bases_ref, terms_ref):
    count = columns_ref.shape[0]
    columns = [columns_ref[index] for index in range(count)]
    for index in range(count):
        vector = columns[index]
        vector = vector * lax.rsqrt(jnp.sum(vector * vector, -1, keepdims=True) + 1e-06)
        bases_ref[index] = vector
        for later in range(index + 1, count):
            other = columns[later]
            columns[later] = other - jnp.sum(vector * other, -1, keepdims=True) * vector
        terms = []
        for _ in range(3):
            terms.append(vector.astype(jnp.bfloat16))
            vector = vector - terms[-1].astype(jnp.float32)
        for place, term in enumerate(left_terms):
            terms_ref[place * count + index] = terms[term].astype(jnp.float32)


def orthonormal_all(lefts):
    longest = max(left.shape[1] for left in lefts)
    padded = jnp.stack(
        [jnp.pad(left, ((0, 0), (0, longest - left.shape[1]))) for left in lefts], 1
    )
    many = len(left_terms) * padded.shape[0]
    bases, terms = pl.pallas_call(
        orthonormal_kernel,
        out_shape=[
            jax.ShapeDtypeStruct(padded.shape, jnp.float32),
            jax.ShapeDtypeStruct((many,) + padded.shape[1:], jnp.float32),
        ],
    )(padded)
    return [bases[:, index, : left.shape[1]] for index, left in enumerate(lefts)], [
        to_low(terms[:, index, : left.shape[1]]) for index, left in enumerate(lefts)
    ]


def outer_terms(rights):
    terms = split_low(rights)
    return jnp.concatenate([terms[term] for term in right_terms], 0)


def coarse(values):
    return lax.reduce_precision(values, 8, 7)


def split_low(values):
    first = coarse(values)
    second = coarse(values - first)
    return [to_low(first), to_low(second), to_low(values - first - second)]


def join_low(terms):
    terms = [term.astype(jnp.float32) for term in terms]
    return terms[0] + (terms[1] + terms[2])


def vocab_tile(shard_rows, most=640):
    tiles = -(-shard_rows // most)
    return -(-(-(-shard_rows // tiles)) // 16) * 16


def head_kernel(shard_rows, rows_ref, table_ref, out_ref, total, stats):
    step = pl.program_id(0)
    tile_rows, wide = table_ref.shape

    @pl.when(step == 0)
    def _():
        total[...] = jnp.zeros_like(total)
        stats[0:1, :] = jnp.full((1, stats.shape[1]), -1e30, jnp.float32)
        stats[1:2, :] = jnp.zeros((1, stats.shape[1]), jnp.float32)

    row_ids = step * tile_rows + lax.broadcasted_iota(jnp.int32, (tile_rows, 1), 0)
    present = row_ids < shard_rows
    tile = jnp.where(present, table_ref[...], 0.0).astype(jnp.bfloat16)
    logits = lax.dot_general(
        tile, rows_ref[...], (((1,), (1,)), ((), ())), preferred_element_type=jnp.float32
    )
    logits = jnp.where(present, logits, -1e30)
    before = stats[0:1, :]
    top = jnp.maximum(before, jnp.max(logits, 0, keepdims=True))
    fade = jnp.exp(before - top)
    expo = jnp.exp(logits - top)
    stats[0:1, :] = top
    stats[1:2, :] = stats[1:2, :] * fade + jnp.sum(expo, 0, keepdims=True)
    total[...] = total[...] * fade + lax.dot_general(
        tile,
        expo.astype(jnp.bfloat16),
        (((0,), (0,)), ((), ())),
        preferred_element_type=jnp.float32,
    )

    @pl.when(step == pl.num_programs(0) - 1)
    def _():
        out_ref[:, :wide] = total[...].T.astype(jnp.bfloat16)
        terms = []
        for index in (0, 1):
            value = stats[index : index + 1, :]
            for _ in range(3):
                part = value.astype(jnp.bfloat16).astype(jnp.float32)
                terms.append(part)
                value = value - part
        spare = jnp.zeros((out_ref.shape[1] - wide - 6, value.shape[1]), jnp.float32)
        out_ref[:, wide:] = jnp.concatenate(terms + [spare], 0).T.astype(jnp.bfloat16)


def head_forward(rows, table):
    count, wide = rows.shape
    shard_rows = table.shape[0]
    tile = vocab_tile(shard_rows, 1280 if count <= 1024 else 640)
    return pl.pallas_call(
        functools.partial(head_kernel, shard_rows),
        grid=(pl.cdiv(shard_rows, tile),),
        in_specs=[
            pl.BlockSpec((count, wide), lambda i: (0, 0)),
            pl.BlockSpec((tile, wide), lambda i: (i, 0)),
        ],
        out_specs=pl.BlockSpec((count, wide + 128), lambda i: (0, 0)),
        out_shape=jax.ShapeDtypeStruct((count, wide + 128), jnp.bfloat16),
        scratch_shapes=[
            pltpu.VMEM((wide, count), jnp.float32),
            pltpu.VMEM((8, count), jnp.float32),
        ],
        compiler_params=pltpu.CompilerParams(vmem_limit_bytes=56 * 2**20),
        cost_estimate=pl.CostEstimate(
            flops=4 * shard_rows * count * wide,
            bytes_accessed=4 * shard_rows * wide,
            transcendentals=shard_rows * count,
        ),
    )(rows, table)


def table_kernel(
    rows_ref, shift_ref, added_ref, ids_ref, table_ref, moment_ref, new_table_ref, new_moment_ref
):
    tile_rows, wide = table_ref.shape
    row_ids = pl.program_id(0) * tile_rows
    row_ids = row_ids + lax.broadcasted_iota(jnp.int32, (tile_rows, 1), 0)
    hits = (row_ids == ids_ref[...]).astype(jnp.bfloat16)
    new_moment_ref[...] = momentum_decay * moment_ref[...] + dense(hits, added_ref[...])
    tile = table_ref[...].astype(jnp.bfloat16)
    chunk = min(512, rows_ref.shape[0])

    def one(spot):
        rows = rows_ref[spot, :wide]
        grad = jnp.exp(dense_last(tile, rows) - shift_ref[0:1, spot])
        return dense(grad.astype(jnp.bfloat16), rows)

    together = 4 * chunk if rows_ref.shape[0] % (4 * chunk) == 0 else chunk

    def some(index, carry):
        begin = pl.multiple_of(index * together, together)
        parts = [one(pl.ds(begin + k * chunk, chunk)) for k in range(together // chunk)]
        new_moment_ref[...] += sum(parts[1:], parts[0])
        return carry

    if rows_ref.shape[0] == together:
        some(0, 0)
    else:
        lax.fori_loop(0, rows_ref.shape[0] // together, some, 0)
    new_table_ref[...] = table_ref[...] - table_rate * new_moment_ref[...]


def table_update(rows, shift, added, ids, table, moment):
    shard_rows, wide = table.shape
    tile = vocab_tile(shard_rows)
    whole = lambda array: pl.BlockSpec(
        array.shape, lambda i: (0, 0), pipeline_mode=pl.Buffered(buffer_count=1)
    )
    part = pl.BlockSpec((tile, wide), lambda i: (i, 0))
    return pl.pallas_call(
        table_kernel,
        grid=(pl.cdiv(shard_rows, tile),),
        in_specs=[whole(rows), whole(shift), whole(added), whole(ids), part, part],
        out_specs=[part, part],
        out_shape=[jax.ShapeDtypeStruct(table.shape, jnp.float32)] * 2,
        compiler_params=pltpu.CompilerParams(vmem_limit_bytes=56 * 2**20),
        cost_estimate=pl.CostEstimate(
            flops=shard_rows * wide * (4 * rows.shape[0] + 2 * ids.shape[1]),
            bytes_accessed=16 * shard_rows * wide,
            transcendentals=shard_rows * rows.shape[0],
        ),
    )(rows, shift, added, ids, table, moment)


def visible_pairs(key_ref, row_ref):
    spots, segs = key_ref[:, 0:1], key_ref[:, 1:2]
    related = (segs == row_ref[1:2, :]) | (segs == row_ref[2:3, :]) | (segs == row_ref[3:4, :])
    return related & (spots <= row_ref[0:1, :])


def head_columns(width, head):
    columns = lax.broadcasted_iota(jnp.int32, (1, width), 1)
    return (columns >= head * HD) & (columns < (head + 1) * HD)


def attend_kernel(
    shard_in,
    emb_ref,
    pack_ref,
    bias_ref,
    key_ref,
    row_ref,
    index_ref,
    x_ref,
    x_rows_ref,
    emb_rows_ref,
    query_ref,
    key_value_ref,
    attn_ref,
    lse_ref,
    in_ref,
):
    length = x_ref.shape[0]
    count, width = query_ref.shape
    block = min(256, length)
    share = pack_ref.shape[1] - 3 * width
    halves = in_ref.shape[1] // share
    for owner in range(in_ref.shape[0] // shard_in):
        for part in range(halves):
            begin = (owner * halves + part) * shard_in
            in_ref[owner * shard_in : (owner + 1) * shard_in, part * share : (part + 1) * share] = (
                pack_ref[begin : begin + shard_in, :share]
            )

    def one_block(index, carry):
        spot = pl.ds(pl.multiple_of(index * block, block), block)
        x_low = to_low(dense(emb_ref[spot, :], in_ref[...]))
        x_ref[spot, :] = x_low
        mixed = dense(x_low, pack_ref[:, share + width :]) + bias_ref[:, width:]
        key_value_ref[spot, :] = to_low(mixed)
        return carry

    lax.fori_loop(0, length // block, one_block, 0)
    chosen = index_ref[...] == lax.broadcasted_iota(jnp.int32, (count, length), 1)
    emb_rows = to_low(dense(chosen.astype(jnp.bfloat16), emb_ref[:length, :]))
    emb_rows_ref[...] = emb_rows
    x_rows = dense(emb_rows, in_ref[...])
    x_rows_ref[...] = x_rows
    queries = to_low(dense(to_low(x_rows), pack_ref[:, share : share + width]) + bias_ref[:, :width])
    query_ref[...] = queries
    keys_all = key_value_ref[:, :width]
    values_turned = key_value_ref[:, width:].T
    blocked = jnp.where(visible_pairs(key_ref, row_ref), 0.0, -1e30)
    features = lax.broadcasted_iota(jnp.int32, (width, 1), 0)
    attended = jnp.zeros((width, count), jnp.float32)
    for head in range(width // HD):
        own = jnp.where(head_columns(width, head), queries, jnp.zeros_like(queries))
        scores = dense_last(keys_all, own) * HD ** (-0.5) + blocked
        top = jnp.max(scores, 0, keepdims=True)
        expo = jnp.exp(scores - top)
        total = jnp.sum(expo, 0, keepdims=True)
        lse_ref[head : head + 1, :] = top + jnp.log(total)
        result = dense(values_turned, to_low(expo / total))
        mine = (features >= head * HD) & (features < (head + 1) * HD)
        attended = jnp.where(mine, result, attended)
    attn_ref[...] = to_low(attended.T)


def attend(id_rows, pack, shard_in, width, bias, key_facts, row_facts, row_index):
    emb_width = id_rows.shape[1]
    model_width = pack.shape[0]
    length = key_facts.shape[0]
    count = row_index.shape[0]
    low = lambda *shape: jax.ShapeDtypeStruct(shape, jnp.bfloat16)
    full = lambda *shape: jax.ShapeDtypeStruct(shape, jnp.float32)
    return pl.pallas_call(
        functools.partial(attend_kernel, shard_in),
        out_shape=[
            low(length, model_width),
            full(count, model_width),
            low(count, emb_width),
            low(count, width),
            low(length, 2 * width),
            low(count, width),
            full(8, count),
            low(emb_width, model_width),
        ],
        compiler_params=pltpu.CompilerParams(vmem_limit_bytes=48 * 2**20),
        cost_estimate=pl.CostEstimate(
            flops=2 * length * model_width * (emb_width + 2 * width) + 4 * length * count * width,
            bytes_accessed=2 * length * (emb_width + model_width + 2 * width),
            transcendentals=length * count * width // HD,
        ),
    )(id_rows, pack, bias, key_facts, row_facts, row_index)


def attend_back_kernel(
    z_ref,
    proj_ref,
    query_ref,
    key_value_ref,
    lse_ref,
    key_ref,
    row_ref,
    pack_ref,
    in_ref,
    pre_ref,
    query_grad_ref,
    key_value_grad_ref,
    x_part_ref,
    row_part_ref,
    emb_part_ref,
):
    count, width = query_ref.shape
    length = key_value_ref.shape[0]
    slots = pre_ref.shape[0]
    share = pack_ref.shape[1] - 3 * width
    scale = HD ** (-0.5)
    queries = query_ref[...]
    keys_all = key_value_ref[:, :width]
    values_all = key_value_ref[:, width:]
    keys_turned = keys_all.T
    attn_grad = to_low(dense(z_ref[...], proj_ref[...]))
    blocked = jnp.where(visible_pairs(key_ref, row_ref), 0.0, -1e30)
    features = lax.broadcasted_iota(jnp.int32, (width, 1), 0)
    key_grad = jnp.zeros((length, width), jnp.float32)
    value_grad = jnp.zeros((length, width), jnp.float32)
    query_grad = jnp.zeros((width, count), jnp.float32)
    for head in range(width // HD):
        mine = head_columns(width, head)
        own = jnp.where(mine, queries, jnp.zeros_like(queries))
        own_grad = jnp.where(mine, attn_grad, jnp.zeros_like(attn_grad))
        scores = dense_last(keys_all, own) * scale + blocked
        probs = jnp.exp(scores - lse_ref[head : head + 1, :])
        probs_grad = dense_last(values_all, own_grad)
        rowdot = jnp.sum(probs * probs_grad, 0, keepdims=True)
        scores_grad = to_low(probs * (probs_grad - rowdot))
        value_grad += dense(to_low(probs), own_grad)
        key_grad += dense(scores_grad, own)
        rows = (features >= head * HD) & (features < (head + 1) * HD)
        query_grad = jnp.where(rows, dense(keys_turned, scores_grad), query_grad)
    query_grad = to_low((query_grad * scale).T)
    query_grad_ref[...] = query_grad
    key_value_grad_ref[:, :width] = to_low(key_grad * scale)
    key_value_grad_ref[:, width:] = to_low(value_grad)
    row_part = dense_last(query_grad, pack_ref[:, share : share + width])
    row_part_ref[:slots, :] = to_low(row_part[:slots] + pre_ref[...])
    row_part_ref[slots:, :] = to_low(row_part[slots:])
    row_emb = to_low(dense_last(row_part_ref[...], in_ref[...]))
    block = min(256, length)

    def one_block(index, carry):
        begin = pl.multiple_of(index * block, block)
        spot = pl.ds(begin, block)
        x_part = to_low(dense_last(key_value_grad_ref[spot, :], pack_ref[:, share + width :]))
        x_part_ref[spot, :] = x_part
        places = begin + lax.broadcasted_iota(jnp.int32, (block, 1), 0)
        chosen = (places == row_ref[4:5, :]).astype(jnp.bfloat16)
        emb_part_ref[spot, :] = to_low(dense_last(x_part, in_ref[...]) + dense(chosen, row_emb))
        return carry

    lax.fori_loop(0, length // block, one_block, 0)


def attend_back(
    z_rows, own_proj_t, queries, key_value, lse, key_facts, row_facts, pack, full_in, pre_grad
):
    count, width = queries.shape
    length = key_value.shape[0]
    emb_width, model_width = full_in.shape
    low = lambda *shape: jax.ShapeDtypeStruct(shape, jnp.bfloat16)
    return pl.pallas_call(
        attend_back_kernel,
        out_shape=[
            low(count, width),
            low(length, 2 * width),
            low(length, model_width),
            low(count, model_width),
            low(length, emb_width),
        ],
        compiler_params=pltpu.CompilerParams(vmem_limit_bytes=48 * 2**20),
        cost_estimate=pl.CostEstimate(
            flops=2 * length * model_width * (emb_width + 2 * width) + 10 * length * count * width,
            bytes_accessed=2 * length * (emb_width + model_width + 2 * width),
            transcendentals=length * count * width // HD,
        ),
    )(z_rows, own_proj_t, queries, key_value, lse, key_facts, row_facts, pack, full_in, pre_grad)


def lookup(codes, table_row):
    hits = codes[:, None] == jnp.arange(table_row.shape[0])[None, :]
    return jnp.sum(jnp.where(hits, table_row[None, :], 0), 1)


def after(values, *others):
    return lax.optimization_barrier((values, *others))[0]


def together(*values):
    return lax.optimization_barrier(values)


def columns_of(values, sizes):
    cuts = [sum(sizes[:i]) for i in range(len(sizes) + 1)]
    return [values[:, cuts[i] : cuts[i + 1]] for i in range(len(sizes))]


def advance(weight, moment, approx, rate):
    fresh_moment = momentum_decay * moment + approx
    return (weight - rate * fresh_moment, fresh_moment)


def per_device(
    tokens,
    segments,
    parents,
    completion,
    targets,
    table,
    table_moment,
    vectors,
    vector_moment,
    w_in,
    moment_in,
    error_in,
    factor_in,
    w_qkv,
    moment_qkv,
    error_qkv,
    factor_qkv,
    w_proj,
    moment_proj,
    error_proj,
    factor_proj,
    w_up,
    moment_up,
    error_up,
    factor_up,
    w_down,
    moment_down,
    error_down,
    factor_down,
    w_out,
    moment_out,
    error_out,
    factor_out,
):
    dp_count = lax.axis_size("dp")
    tensor_count = lax.axis_size("tensor")
    dp_index = lax.axis_index("dp")
    tensor_index = lax.axis_index("tensor")
    token_ids = tokens[0]
    comp_row = completion[0]
    target_row = targets[0]
    local_count = token_ids.shape[0]
    slots = comp_row.shape[0]
    segs = segments[0]
    length = segs.shape[0]
    shard_rows, emb_width = table.shape
    vocab_start = dp_index * shard_rows
    width = w_qkv.shape[2]
    hidden_share = w_up.shape[1]
    model_width = vectors.shape[1]
    heads_here = width // HD
    scale = HD ** (-0.5)
    shard_width = w_qkv.shape[0]
    blocks = range(tensor_count)

    halves = shard_width // w_in.shape[0]
    share_in = model_width // halves
    in_low = to_low(w_in)
    in_stack = jnp.concatenate(
        [in_low[:, h * share_in : (h + 1) * share_in] for h in range(halves)], 0
    )
    qkv_low = to_low(w_qkv).reshape(shard_width, 3 * width)
    pack_first = lax.all_gather(
        jnp.concatenate([in_stack, qkv_low], 1), "dp", axis=0, tiled=True
    )
    pack_second = lax.all_gather(
        jnp.concatenate([to_low(w_proj).T, to_low(w_up)], 1), "dp", axis=0, tiled=True
    )
    pack_third = lax.all_gather(
        jnp.concatenate([to_low(w_down).T, to_low(w_out)], 1), "dp", axis=0, tiled=True
    )
    full_proj_t = pack_second[:, :width]
    full_up = pack_second[:, width:]
    full_down_t = pack_third[:, :hidden_share]
    full_out = pack_third[:, hidden_share:]

    meta = jnp.stack(gather_blocks(jnp.concatenate([token_ids, comp_row, target_row]), "tensor"))
    comp_tree = meta[:, local_count : local_count + slots]
    ids = jnp.concatenate(
        [meta[:, :local_count].reshape(-1), meta[:, local_count + slots :].reshape(-1)]
    )

    id_count = ids.shape[0]
    share = -(-id_count // (16 * dp_count)) * 16
    owner = (ids // shard_rows) ^ dp_index
    order = jnp.arange(id_count)
    before = order[None, :] < order[:, None]
    same = ids[:, None] == ids[None, :]
    first_one = ~jnp.any(same & before, 1)
    rank = jnp.sum((owner[:, None] == owner[None, :]) & before & first_one[None, :], 1)
    rank = jnp.sum(jnp.where(same & first_one[None, :], rank[None, :], 0), 1)
    rounds_here = jnp.max(rank) // share + 1

    def listed(turn):
        place = rank - turn * share
        place = jnp.where((place >= 0) & (place < share), owner * share + place, -1)
        hits = place[None, :] == jnp.arange(dp_count * share)[:, None]
        entries = jnp.max(jnp.where(hits, ids[None, :], -1), 1)
        return hits.astype(jnp.bfloat16), entries.reshape(dp_count, share)

    def fetch(asked, kind):
        spots = jnp.clip(asked - vocab_start, 0, shard_rows - 1)
        picked = jnp.take(table, spots.reshape(-1), axis=0).astype(kind).reshape(dp_count, share, -1)
        return jnp.concatenate(exchange_blocks([picked[s] for s in range(dp_count)], "dp"), 0)

    hits_first, entries = listed(0)
    notes = [jnp.concatenate([entries[s], rounds_here[None]]) for s in range(dp_count)]
    notes = jnp.stack(exchange_blocks(notes, "dp"))
    asked_first = notes[:, :share]
    rounds = jnp.max(notes[:, share])

    def fetch_more(turn, rows):
        hits, entries = listed(turn)
        asked = jnp.stack(exchange_blocks([entries[s] for s in range(dp_count)], "dp"))
        return rows + to_low(dense_first(hits, to_low(coarse(fetch(asked, jnp.float32)))))

    id_rows = to_low(dense_first(hits_first, fetch(asked_first, jnp.bfloat16)))
    id_rows = lax.fori_loop(1, rounds, fetch_more, id_rows)
    emb_all = id_rows[:length]
    target_rows = id_rows[length : length + slots].astype(jnp.float32)

    starts = [(tensor_index ^ s) * local_count for s in blocks]
    key_spots = jnp.concatenate([start + jnp.arange(local_count) for start in starts])
    key_segs = jnp.concatenate([lax.dynamic_slice_in_dim(segs, a, local_count) for a in starts])
    slot_local = [
        jnp.clip(comp_tree[s] - starts[s], 0, local_count - 1) for s in blocks
    ]
    row_index = jnp.concatenate([s * local_count + slot_local[s] for s in blocks])
    row_spots = jnp.concatenate([starts[s] + slot_local[s] for s in blocks])
    chosen = row_index[:, None] == jnp.arange(length)[None, :]
    row_segs = jnp.sum(jnp.where(chosen, key_segs[None, :], 0), 1)
    row_first = lookup(row_segs, parents[0])
    row_second = lookup(row_first, parents[0])
    key_facts = jnp.stack([key_spots, key_segs], 1)
    row_facts = jnp.stack(
        [row_spots, row_segs, row_first, row_second, row_index] + [jnp.zeros_like(row_index)] * 3
    )
    bias_query = lax.dynamic_slice_in_dim(vectors[4], tensor_index * width, width)
    bias_value = lax.dynamic_slice_in_dim(vectors[5], tensor_index * width, width)
    bias = jnp.concatenate([bias_query, jnp.zeros_like(bias_query), bias_value])[None]
    x_low, x_rows, emb_rows, queries, key_value, attn_low, lse_keys, full_in = attend(
        id_rows, pack_first, w_in.shape[0], width, bias, key_facts, row_facts, row_index[:, None]
    )
    z_part = to_low(dense_last(attn_low, full_proj_t))
    z_branch = add_up(
        exchange_blocks([z_part[s * slots : (s + 1) * slots] for s in blocks], "tensor")
    )
    pre_one = x_rows[:slots] + z_branch + vectors[6]
    h_one = layer_norm(pre_one, vectors[0], vectors[1])
    h_rows = jnp.concatenate(gather_blocks(to_low(h_one), "tensor"), 0)
    bias_up = lax.dynamic_slice_in_dim(
        vectors[8:].reshape(-1), tensor_index * hidden_share, hidden_share
    )
    upper = dense(h_rows, full_up) + bias_up
    act_low = to_low(gelu_tanh(upper))
    f_part = to_low(dense_last(act_low, full_down_t))
    f_branch = add_up(
        exchange_blocks([f_part[s * slots : (s + 1) * slots] for s in blocks], "tensor")
    )
    pre_two = h_one + f_branch + vectors[7]
    h_two = layer_norm(pre_two, vectors[2], vectors[3])
    h_two_low = to_low(h_two)
    rows_low = to_low(dense(h_two_low, full_out))

    h_two_rows = gather_blocks(jnp.concatenate([h_two_low, rows_low], 1), "tensor")
    h_two_rows = jnp.concatenate(h_two_rows, 0)
    tree_rows = h_two_rows[:, model_width:]
    h_two_rows = h_two_rows[:, :model_width]
    rows_group = lax.all_gather(rows_low, "dp", axis=0, tiled=True)
    rows_group, tree_rows, h_two_rows = lax.optimization_barrier(
        (rows_group, tree_rows, h_two_rows)
    )
    parts = head_forward(rows_group, table)
    parts = lax.all_to_all(parts, "dp", 0, 0, tiled=True).reshape(dp_count, slots, -1)
    part_tops = join_low([parts[:, :, emb_width + i] for i in range(3)])
    part_sums = join_low([parts[:, :, emb_width + 3 + i] for i in range(3)])
    head_top = jnp.max(part_tops, 0)
    shares = jnp.exp(part_tops - head_top)
    total = jnp.sum(shares * part_sums, 0)
    lse = head_top + jnp.log(total)
    valid = comp_row >= 0
    target_logits = jnp.sum(rows_low.astype(jnp.float32) * target_rows, -1)
    loss_part = jnp.sum(jnp.where(valid, lse - target_logits, 0.0))
    slot_weight = 1.0 / (dp_count * tensor_count * slots)
    weight = jnp.where(valid, slot_weight, 0.0)
    mean = add_up(
        [parts[s, :, :emb_width] * (shares[s] / total)[:, None] for s in range(dp_count)]
    )
    out_low = to_low((mean - target_rows) * weight[:, None])

    shift = jnp.where(valid, lse - jnp.log(slot_weight), 1e30)
    shift = jnp.pad(jnp.stack(split_low(shift), 1), ((0, 0), (0, 125)))

    h_two_grad = dense_last(out_low, full_out)
    norm_two = jax.vjp(layer_norm, pre_two, vectors[2], vectors[3])[1]
    pre_two_grad, gain_two_grad, shift_two_grad = norm_two(h_two_grad)
    f_rows = gather_blocks(jnp.concatenate([to_low(pre_two_grad), shift], 1), "tensor")
    f_rows = jnp.concatenate(f_rows, 0)
    rows_all = lax.all_gather(
        jnp.concatenate([tree_rows, f_rows[:, model_width:]], 1), "dp", axis=0, tiled=True
    )
    shift_all = join_low([rows_all[:, emb_width + i] for i in range(3)])[None]
    f_rows = f_rows[:, :model_width]
    grad_down = dense_first(act_low, f_rows)
    act_grad = dense(f_rows, full_down_t)
    upper_low = to_low(jax.vjp(gelu_tanh, upper)[1](act_grad)[0])
    grad_up = dense_first(h_rows, upper_low)
    h_part = to_low(dense_last(upper_low, full_up))
    h_parts = exchange_blocks([h_part[s * slots : (s + 1) * slots] for s in blocks], "tensor")
    early = (3, 4)
    early_merged = [grad_up + error_up[0], grad_down + error_down[0]]
    early_lefts = [left_factor(*pair) for pair in zip(early_merged, (factor_up, factor_down[0]))]
    early_sizes = [left.shape[1] for left in early_lefts]
    early_lefts = jnp.concatenate(early_lefts, 1)
    h_parts[0], early_lefts = together(h_parts[0], early_lefts)
    h_one_grad = pre_two_grad + add_up(h_parts)
    norm_one = jax.vjp(layer_norm, pre_one, vectors[0], vectors[1])[1]
    pre_one_grad, gain_one_grad, shift_one_grad = norm_one(h_one_grad)
    z_low = to_low(pre_one_grad)
    z_rows = gather_blocks(jnp.concatenate([z_low, out_low], 1), "tensor")
    early_lefts = summed_over(early_lefts, "dp")
    z_rows[0], early_lefts = together(z_rows[0], early_lefts)
    z_rows = jnp.concatenate(z_rows, 0)
    grad_out = dense_first(h_two_rows, z_rows[:, model_width:])
    z_rows = z_rows[:, :model_width]
    grad_proj = dense_first(attn_low, z_rows)
    query_grad, key_value_grad, x_part, row_part, emb_part = attend_back(
        z_rows,
        full_proj_t,
        queries,
        key_value,
        lse_keys,
        key_facts,
        row_facts,
        pack_first,
        full_in,
        pre_one_grad,
    )
    x_rows_low = to_low(x_rows)
    value_grad = key_value_grad[:, width:]
    grad_query = dense_first(x_rows_low, query_grad)
    grad_key = dense_first(x_low, key_value_grad[:, :width])
    grad_value = dense_first(x_low, value_grad)

    grad_in = dense_first(emb_all, x_part) + dense_first(emb_rows, row_part)
    emb_parts = exchange_blocks(
        [emb_part[s * local_count : (s + 1) * local_count] for s in blocks], "tensor"
    )
    def placed(values, size, total_size):
        return lax.dynamic_update_slice_in_dim(
            jnp.zeros((total_size,), jnp.float32), values, tensor_index * size, 0
        )

    head_rows = jnp.stack(
        [
            gain_one_grad,
            shift_one_grad,
            gain_two_grad,
            shift_two_grad,
            placed(jnp.sum(query_grad.astype(jnp.float32), 0), width, model_width),
            placed(jnp.sum(value_grad.astype(jnp.float32), 0), width, model_width),
            jnp.sum(pre_one_grad, 0),
            jnp.sum(pre_two_grad, 0),
        ]
    )
    up_rows = placed(
        jnp.sum(upper_low.astype(jnp.float32), 0), hidden_share, hidden_share * tensor_count
    ).reshape(-1, model_width)
    loss_row = jnp.full((1, model_width), loss_part)
    vector_part = jnp.concatenate([head_rows, up_rows, loss_row], 0)

    merged = (
        grad_in + error_in[0] * (1.0 / tensor_count),
        None,
        grad_proj + error_proj[0],
    ) + tuple(early_merged) + (grad_out + error_out[0],)
    factors = (
        factor_in,
        factor_qkv.reshape(3 * width, -1),
        factor_proj[0],
        None,
        None,
        factor_out,
    )
    bases = [None] * 6
    fresh = [None] * 6
    parts_of = [None] * 6
    merged_qkv = [
        grad + error_qkv[0, :, part]
        for part, grad in enumerate((grad_query, grad_key, grad_value))
    ]
    late = (0, 1, 2, 5)
    lefts = [
        sum(left_factor(merged_qkv[part], factor_qkv[part]) for part in range(3))
        if index == 1
        else left_factor(merged[index], factors[index])
        for index in late
    ]
    sizes = [left.shape[1] for left in lefts] + [vector_part.size // lefts[0].shape[0]]
    lefts = jnp.concatenate(lefts + [vector_part.reshape(lefts[0].shape[0], -1)], 1)
    early_bases, early_terms = orthonormal_all(columns_of(early_lefts, early_sizes))
    early_rights = [right_factor(*pair) for pair in zip(early_merged, early_bases)]
    early_sizes = [right.shape[1] for right in early_rights]
    early_rights = jnp.concatenate(early_rights, 1)
    emb_parts[0], lefts, early_rights = together(emb_parts[0], lefts, early_rights)
    emb_grad_own = to_low(add_up(emb_parts))
    emb_grad = gather_blocks(emb_grad_own, "tensor")
    lefts = summed_over(lefts, "dp")
    early_rights = summed_over(early_rights, "dp")
    emb_grad[0], lefts, early_rights = together(emb_grad[0], lefts, early_rights)
    emb_grad = jnp.concatenate(emb_grad, 0)
    early_parts = columns_of(outer_terms(early_rights), early_sizes)
    early_rights = columns_of(early_rights, early_sizes)

    def error_left(index):
        return merged[index] - dense_first(bases[index], parts_of[index]) * (1.0 / dp_count)

    errors_new = [None] * 6
    for i, index in enumerate(early):
        bases[index] = early_terms[i]
        fresh[index] = early_rights[i]
        parts_of[index] = early_parts[i]
        errors_new[index] = error_left(index)
    lefts = columns_of(lefts, sizes)
    flat = after(jnp.concatenate([lefts[0], lefts[-1]], 1), emb_grad)
    flat = add_pairs(gather_blocks(flat, "tensor"))
    lefts[0] = flat[:, : sizes[0]]
    vector_sum = flat[:, sizes[0] :].reshape(vector_part.shape)
    found_bases, found_terms = orthonormal_all(lefts[:-1])
    rights = [
        jnp.concatenate([right_factor(merged_qkv[part], found_bases[i]) for part in range(3)], 1)
        if index == 1
        else right_factor(merged[index], found_bases[i])
        for i, index in enumerate(late)
    ]
    sizes = [right.shape[1] for right in rights]
    rights = summed_over(jnp.concatenate(rights, 1), "dp")
    grad_in_own = lax.psum_scatter(
        after(to_low(grad_in), emb_grad), "tensor", scatter_dimension=0, tiled=True
    )
    tree_weight = jnp.where(comp_tree.reshape(-1) >= 0, slot_weight, 0.0)
    target_grad = to_low(tree_rows.astype(jnp.float32) * -tree_weight[:, None])
    id_grad = jnp.concatenate([emb_grad, target_grad], 0)

    def deliver(hits):
        listed_rows = to_low(dense(hits, id_grad)).reshape(dp_count, share, -1)
        rows = exchange_blocks([listed_rows[s] for s in range(dp_count)], "dp")
        return jnp.concatenate(rows, 0)

    def deliver_more(turn, state):
        hits, entries = listed(turn)
        asked = jnp.stack(exchange_blocks([entries[s] for s in range(dp_count)], "dp"))
        spots = asked.reshape(-1) - vocab_start
        rows = deliver(hits).astype(jnp.float32)
        rows = jnp.where((spots >= 0)[:, None], rows, 0.0)
        spots = jnp.clip(spots, 0, shard_rows - 1)
        return state[0].at[spots].add(-table_rate * rows), state[1].at[spots].add(rows)

    added, rights, errors_new[3], errors_new[4], grad_in_own = together(
        deliver(hits_first), rights, errors_new[3], errors_new[4], grad_in_own
    )
    updated = list(table_update(
        rows_all, shift_all, added, asked_first.reshape(1, -1) - vocab_start, table, table_moment
    ))
    right_in = gather_blocks(rights[:, : sizes[0]], "tensor")
    grad_in_sum = lax.all_gather(grad_in_own, "tensor", axis=0, tiled=True)
    right_in[0], updated[0] = together(right_in[0], updated[0])
    new_table, new_table_moment = lax.fori_loop(1, rounds, deliver_more, tuple(updated))
    rights = columns_of(rights, sizes)
    rights[0] = add_pairs(right_in)
    right_parts = columns_of(outer_terms(jnp.concatenate(rights, 1)), sizes)
    for i, index in enumerate(late):
        bases[index] = found_terms[i]
        fresh[index] = rights[i]
        parts_of[index] = right_parts[i]
    merged = (grad_in_sum.astype(jnp.float32) + error_in[0],) + merged[1:]
    for index in (0, 2, 5):
        errors_new[index] = error_left(index)
    errors_new[1] = jnp.stack(
        [
            merged_qkv[part]
            - dense_first(bases[1], parts_of[1][:, part * width : (part + 1) * width])
            * (1.0 / dp_count)
            for part in range(3)
        ],
        0,
    ).transpose(1, 0, 2)

    def shard(index, size, axis):
        left, right = bases[index], parts_of[index]
        if axis == 0:
            left = lax.dynamic_slice_in_dim(left, dp_index * size, size, 1)
        else:
            right = lax.dynamic_slice_in_dim(right, dp_index * size, size, 1)
        return dense_first(left, right)

    shard_in = shard(0, w_in.shape[0], 0)
    shard_qkv = shard(1, shard_width, 0)
    shard_qkv = jnp.stack(
        [shard_qkv[:, part * width : (part + 1) * width] for part in range(3)], 1
    )
    shard_proj = shard(2, w_proj.shape[1], 1)
    shard_up = shard(3, w_up.shape[0], 0)
    shard_down = shard(4, w_down.shape[1], 1)
    shard_out = shard(5, w_out.shape[0], 0)
    fresh = [values.T for values in fresh]
    loss_sum = vector_sum[-1, 0]
    vector_grad = vector_sum[:-1]
    new_w_in, new_moment_in = advance(w_in, moment_in, shard_in, matrix_rates[0])
    new_w_qkv, new_moment_qkv = advance(w_qkv, moment_qkv, shard_qkv, matrix_rates[1])
    new_w_proj, new_moment_proj = advance(w_proj, moment_proj, shard_proj, matrix_rates[2])
    new_w_up, new_moment_up = advance(w_up, moment_up, shard_up, matrix_rates[3])
    new_w_down, new_moment_down = advance(w_down, moment_down, shard_down, matrix_rates[4])
    new_w_out, new_moment_out = advance(w_out, moment_out, shard_out, matrix_rates[5])
    new_vectors, new_vector_moment = advance(vectors, vector_moment, vector_grad, vector_rate)
    return (
        loss_sum,
        new_table,
        new_table_moment,
        new_vectors,
        new_vector_moment,
        new_w_in,
        new_moment_in,
        errors_new[0][None],
        fresh[0],
        new_w_qkv,
        new_moment_qkv,
        errors_new[1].reshape(1, model_width, 3, width),
        fresh[1].reshape(3, width, -1),
        new_w_proj,
        new_moment_proj,
        errors_new[2][None],
        fresh[2][None],
        new_w_up,
        new_moment_up,
        errors_new[3][None],
        fresh[3],
        new_w_down,
        new_moment_down,
        errors_new[4][None],
        fresh[4][None],
        new_w_out,
        new_moment_out,
        errors_new[5][None],
        fresh[5],
    )


def solution(mesh):
    return jax.shard_map(
        per_device,
        mesh=mesh,
        in_specs=(
            P("dp", "tensor"),
            P("dp", None),
            P("dp", None),
            P("dp", "tensor"),
            P("dp", "tensor"),
            P("dp", None),
            P("dp", None),
            P(),
            P(),
            P("dp", None),
            P("dp", None),
            P("dp", None, None),
            P(),
            P("dp", None, "tensor"),
            P("dp", None, "tensor"),
            P("dp", None, None, "tensor"),
            P(None, "tensor", None),
            P("tensor", "dp"),
            P("tensor", "dp"),
            P("dp", "tensor", None),
            P("tensor", None, None),
            P("dp", "tensor"),
            P("dp", "tensor"),
            P("dp", None, "tensor"),
            P("tensor", None),
            P("tensor", "dp"),
            P("tensor", "dp"),
            P("dp", "tensor", None),
            P("tensor", None, None),
            P("dp", None),
            P("dp", None),
            P("dp", None, None),
            P(),
        ),
        out_specs=(
            P(),
            P("dp", None),
            P("dp", None),
            P(),
            P(),
            P("dp", None),
            P("dp", None),
            P("dp", None, None),
            P(),
            P("dp", None, "tensor"),
            P("dp", None, "tensor"),
            P("dp", None, None, "tensor"),
            P(None, "tensor", None),
            P("tensor", "dp"),
            P("tensor", "dp"),
            P("dp", "tensor", None),
            P("tensor", None, None),
            P("dp", "tensor"),
            P("dp", "tensor"),
            P("dp", None, "tensor"),
            P("tensor", None),
            P("tensor", "dp"),
            P("tensor", "dp"),
            P("dp", "tensor", None),
            P("tensor", None, None),
            P("dp", None),
            P("dp", None),
            P("dp", None, None),
            P(),
        ),
        check_vma=False,
    )
```

time: 2330 us -> 509 us (0.22)
  waiting for transfers between devices: 1420 us -> 129 us
  other arithmetic: 466 us -> 40 us
  matrix products: 203 us -> 73.1 us
  starting transfers between devices: 1.77 us -> 88.5 us
  Pallas kernels: 0 us -> 84.5 us
  blocking collectives: 79.3 us -> 11.5 us
  local copies, waits for them, and re-layouts: 92.7 us -> 52 us
  between operations: 49.3 us -> 18.8 us
    psum x3 -> x0, waiting for transfers between devices: 600 us -> none  [the longest x1 534 us: per_device(): lax.psum((table_grad, grad_in, grad_out, vector_part, loss_part), 'tensor')]
    all_gather x11 -> x5, waiting for transfers between devices: 494 us -> 0.06 us  [the longest x1 0.02 us: per_device(): lax.all_gather(jnp.concatenate([in_stack, qkv_low], 1), 'dp', axis=0, til...]
    reduce_scatter x5 -> x1, waiting for transfers between devices: 327 us -> 0.02 us  [per_device(): lax.psum_scatter(after(to_low(grad_in), emb_grad), 'tensor', scatter_dime...]
    reduce_sum x97 -> x9, other arithmetic: 238 us -> 4.71 us  [the longest x1 2.34 us: per_device(): jnp.sum((owner[:, None] == owner[None, :]) & before & first_one[None, :], 1)]
    ppermute x0 -> x69, waiting for transfers between devices: none -> 118 us  [swap(): lax.ppermute(values, axis, [(i, i ^ step) for i in range(lax.axis_size(ax...]
    mul x8 -> x0, other arithmetic: 109 us -> none  [the longest x6 109 us: orthonormal(): vector = vector * lax.rsqrt(jnp.sum(vector * vector) + 1e-06)]
    dot_general x35 -> x16, matrix products: 116 us -> 16.8 us  [the longest x8 9.36 us: right_factor(): lax.dot_general(basis, merged, (((1,), (0,)), ((), ())), precision=lax.Pr...]
    pallas_call x0 -> x6, Pallas kernels: none -> 84.5 us  [the longest x1 42.6 us: table_update(): pl.pallas_call(table_kernel, grid=(pl.cdiv(shard_rows, tile),), in_specs=...]
  transfers between devices with their start and end apart: 19 -> 76, of which waited for: 17 -> 28; matrix products, arithmetic and copies ran while one was open for 6% -> 22% of each run, Pallas kernels for 0% -> 12%
where the time goes in v1:
time: 509 us; the launch traced here: 499 us
  waiting for transfers between devices  129 us (25%)
  starting transfers between devices  88.5 us (17%)
  Pallas kernels  84.5 us (17%)
  matrix products  73.1 us (14%)
  local copies, waits for them, and re-layouts  52 us (10%)
  other arithmetic  40 us (8%)
  between operations  18.8 us (4%)
  blocking collectives  11.5 us (2%)
    ppermute x69, waiting for transfers between devices, swap(): lax.ppermute(values, axis, [(i, i ^ step) for i in range(lax.axis_size(ax...  118 us
    ppermute x69, starting transfers between devices, swap(): lax.ppermute(values, axis, [(i, i ^ step) for i in range(lax.axis_size(ax...  83.7 us
    pallas_call x1, Pallas kernels, table_update(): pl.pallas_call(table_kernel, grid=(pl.cdiv(shard_rows, tile),), in_specs=...  42.6 us
    dot_general x24, matrix products, dense_first(): lax.dot_general(left, right, (((0,), (0,)), ((), ())), preferred_element_...  40.3 us
    unnamed x248, local copies, waits for them, and re-layouts  21.9 us
    pallas_call x1, Pallas kernels, head_forward(): pl.pallas_call(functools.partial(head_kernel, shard_rows), grid=(pl.cdiv(...  14.7 us
    all_gather x1, blocking collectives, per_device(): rows_group = lax.all_gather(rows_low, 'dp', axis=0, tiled=True)  11.5 us
    pallas_call x1, Pallas kernels, attend_back(): pl.pallas_call(attend_back_kernel, out_shape=[low(count, width), low(leng...  11.4 us
  transfers between devices with their start and end apart: 76, of which 28 were waited for; matrix products, arithmetic and copies ran while one was open for 22% of the time, Pallas kernels for 12%

profile of v1, /device:TPU:0, one launch (start us, length us, event | category | flops | bytes accessed | tf_op | source)
XLA Modules:
  0.0 499.2 jit_solution(5431480386637416039)
XLA Ops:
  11.7 5.1 %collective-permute-start.30 = (s32[384]{0:T(512)S(1)}, s32[384]{0:T(512)S(1)}, u32[]{:S(2)}, u32[]{:S(2)}) collective-permute-start(s32[384]{0:T(512)S(1)} %pad_add_fusion.4), channel_id=1, source_target_pairs={{0,3},{1,2},{2,1},{3,0},{4,7},{5,6},{6,5},{7,4},{8,11},{9,10},{10,... | collective-permute-start | bytes 4616 | tf_op jit(solution)/shard_map/ppermute | solution.py:62
  41.6 8.9 %gather_fusion.1 = bf16[1280,512]{1,0:T(8,128)(2,1)S(1)} fusion(f32[6284,512]{1,0:T(8,128)} %table_ref.3, s32[2048]{0:T(1024)S(1)} %pad_clamp_fusion.1), kind=kCustom, calls=%fused_computation.1 | custom fusion | bytes 2626560 | tf_op jit(solution)/shard_map/jit(_take)/gather | solution.py:599
  57.6 4.5 collective-permute-done.39
  66.2 7.6 %collective-permute-done.42 = bf16[160,512]{1,0:T(8,128)(2,1)S(1)} collective-permute-done((bf16[160,512]{1,0:T(8,128)(2,1)S(1)}, bf16[160,512]{1,0:T(8,128)(2,1)S(1)}, u32[]{:S(2)}, u32[]{:S(2)}) %collective-permute-start.42) | collective-permute-done | bytes 163872 | tf_op jit(solution)/shard_map/ppermute | solution.py:62
  75.8 4.3 fusion.24
  81.1 9.5 %shard_map.536 = (bf16[1024,1024]{1,0:T(8,128)(2,1)}, f32[256,1024]{1,0:T(8,128)S(1)}, bf16[256,512]{1,0:T(8,128)(2,1)S(1)}, bf16[256,256]{1,0:T(8,128)(2,1)S(1)...) custom-call(bf16[1280,512]{1,0:T(8,128)(2,1)} %get-tuple-element.162, ...), custom_call_target="tpu_custom_call" | custom-call | flops 2415919104 | bytes 4194304 | tf_op jit(solution)/shard_map/pallas_call | solution.py:359
  99.3 4.2 collective-permute-done.47
  103.5 6.6 %collective-permute-done.46 = bf16[64,1024]{1,0:T(8,128)(2,1)} collective-permute-done((bf16[64,1024]{1,0:T(8,128)(2,1)}, bf16[64,1024]{1,0:T(8,128)(2,1)}, u32[]{:S(2)}, u32[]{:S(2)}) %collective-permute-start.46) | collective-permute-done | bytes 131104 | tf_op jit(solution)/shard_map/ppermute | solution.py:62
  116.7 4.0 collective-permute-done.50
  120.7 4.3 collective-permute-done.49
  125.0 3.5 fusion.45
  135.9 3.9 collective-permute-done.53
  139.7 4.9 collective-permute-done.52
  151.6 11.5 %all_gather.21.rows_ref = bf16[512,512]{1,0:T(8,128)(2,1)} all-gather(bf16[64,512]{1,0:T(8,128)(2,1)S(1)} %get-tuple-element.403), channel_id=1, replica_groups=mesh['dp'=8,'tensor'=4] {'dp'}, dimensions={0}, use_global_device_ids=true | all-gather | bytes 589824 | tf_op jit(solution)/shard_map/all_gather | solution.py:665
  166.8 14.7 %shard_map.537 = bf16[512,640]{1,0:T(8,128)(2,1)} custom-call(bf16[512,512]{1,0:T(8,128)(2,1)} %all_gather.21.rows_ref, f32[6284,512]{1,0:T(8,128)} %get-tuple-element.672), custom_call_target="tpu_custom_call" | custom-call | flops 6589251584 | bytes 12869632 | tf_op jit(solution)/shard_map/pallas_call | solution.py:203
  181.6 4.2 all-to-all-start
  186.0 10.9 %all-to-all-done = bf16[8,64,640]{2,1,0:T(8,128)(2,1)} async-done(((bf16[8,64,640]{2,1,0:T(8,128)(2,1)}), bf16[8,64,640]{2,1,0:T(8,128)(2,1)}, u32[]{:S(2)}, u32[]{:S(2)}) %all-to-all-start) | async-done | bytes 655392 | tf_op jit(solution)/shard_map/all_to_all | solution.py:670
  208.3 3.4 collective-permute-done.59
  211.7 4.5 collective-permute-done.58
  251.1 3.5 fusion.137
  260.6 11.4 %shard_map.538 = (bf16[256,256]{1,0:T(8,128)(2,1)S(1)}, bf16[1024,512]{1,0:T(8,128)(2,1)S(1)}, bf16[1024,1024]{1,0:T(8,128)(2,1)}, bf16[256,1024]{1,0:T(8,128)(2,1)S(1)}, bf16[1024,512]{1,0:T(8,128)(2,1)S(1)}) custom-call(bf16[256,1024]{1,0:T(8,128)(2,1)S(1)} %slice.861.z_ref, bf16[1024,256]{1,0:T(8,128)(2,1)S(1)} %slice.830.proj_ref, ...), custom_call_target="tpu_custom_call" | custom-call | flops 2818572288 | bytes 4194304 | tf_op jit(solution)/shard_map/pallas_call | solution.py:455
  281.4 4.3 fusion.223
  297.5 4.6 collective-permute-done.73
  303.9 15.6 %collective-permute-done.70 = bf16[256,512]{1,0:T(8,128)(2,1)S(1)} collective-permute-done((bf16[256,512]{1,0:T(8,128)(2,1)S(1)}, bf16[256,512]{1,0:T(8,128)(2,1)S(1)}, u32[]{:S(2)}, u32[]{:S(2)}) %collective-permute-start.70) | collective-permute-done | bytes 262176 | tf_op jit(solution)/shard_map/ppermute | solution.py:62
  320.7 3.5 collective-permute-done.76
  331.1 15.3 %collective-permute-done.79 = bf16[256,512]{1,0:T(8,128)(2,1)S(1)} collective-permute-done((bf16[256,512]{1,0:T(8,128)(2,1)S(1)}, bf16[256,512]{1,0:T(8,128)(2,1)S(1)}, u32[]{:S(2)}, u32[]{:S(2)}) %collective-permute-start.79) | collective-permute-done | bytes 262176 | tf_op jit(solution)/shard_map/ppermute | solution.py:62
  353.4 5.3 %multiply_subtract_fusion.1 = f32[1024,1024]{1,0:T(8,128)} fusion(f32[1024,1024]{1,0:T(8,128)} %copy-done.7, bf16[48,1,1024]{2,1,0:T(2,128)(2,1)S(1)} %get-tuple-element.348, bf16[48,2048]{1,0:T(8,128)(2,1)S(1)} %constant_dynamic-update-slice_fusion.42), kind=kOutput, calls=%fused_computation.69 | convolution fusion | flops 102760448 | bytes 8683520 | tf_op jit(solution)/shard_map/dot_general | solution.py:28
  364.2 4.7 collective-permute-start.82
  374.7 3.8 collective-permute-done.82
  411.3 7.3 %collective-permute-done.92 = f32[8,3328]{1,0:T(8,128)S(1)} collective-permute-done((f32[8,3328]{1,0:T(8,128)S(1)}, f32[8,3328]{1,0:T(8,128)S(1)}, u32[]{:S(2)}, u32[]{:S(2)}) %collective-permute-start.92) | collective-permute-done | bytes 106528 | tf_op jit(solution)/shard_map/ppermute | solution.py:62
  424.1 3.4 collective-permute-start.95
  433.3 42.6 %shard_map.541 = (f32[6284,512]{1,0:T(8,128)}, f32[6284,512]{1,0:T(8,128)}) custom-call(bf16[2048,640]{1,0:T(8,128)(2,1)} %all-gather.12.cloned.1.call-done.rows_ref, f32[1,2048]{1,0:T(1,128)} %bitcast.448, bf16[1280,512]{1,0:T(8,128)(2,1)} %copy-done.94, s32[1,1280]{1,0:T(1,128)} %sub.252.ids_ref, f32[6284,512]{1,0:T(8,128)} %get-tuple-element.672, ...), custom_call_target="tpu_custom_call" | custom-call | flops 34593570816 | bytes 51478528 | tf_op jit(solution)/shard_map/pallas_call | solution.py:263
  (644 shorter events, 234.6 us)
Async XLA Ops:
  7.2 73.9 %all-gather.6.cloned.1.call-start = ((), (), s32[]{:S(2)}) async-start(), calls=%async_computation.2 | async-start | bytes 2949120 | tf_op jit(solution)/shard_map/all_gather | solution.py:559
  10.5 81.1 %all-gather.8.cloned.1.call-start = ((), (), s32[]{:S(2)}) async-start(), calls=%async_computation.3 | async-start | bytes 2949120 | tf_op jit(solution)/shard_map/all_gather | solution.py:562
  11.5 117.0 %all-gather.10.cloned.1.call-start = ((), (), s32[]{:S(2)}) async-start(), calls=%async_computation.4 | async-start | bytes 3538944 | tf_op jit(solution)/shard_map/all_gather | solution.py:565
  55.1 18.7 %collective-permute-start.42 = (bf16[160,512]{1,0:T(8,128)(2,1)S(1)}, bf16[160,512]{1,0:T(8,128)(2,1)S(1)}, u32[]{:S(2)}, u32[]{:S(2)}) collective-permute-start(bf16[160,512]{1,0:T(8,128)(2,1)S(1)} %get-tuple-element.312), channel_id=1, source_target_pairs={{0,20},{4,16},{8,28},{12,24},{16,4},{20,0},{24,12},{28,8},{1,21},{... | collective-permute-start | bytes 491528 | tf_op jit(solution)/shard_map/ppermute | solution.py:62
  57.1 17.4 %collective-permute-start.43 = (bf16[160,512]{1,0:T(8,128)(2,1)S(1)}, bf16[160,512]{1,0:T(8,128)(2,1)S(1)}, u32[]{:S(2)}, u32[]{:S(2)}) collective-permute-start(bf16[160,512]{1,0:T(8,128)(2,1)S(1)} %get-tuple-element.311), channel_id=1, source_target_pairs={{0,24},{4,28},{8,16},{12,20},{16,8},{20,12},{24,0},{28,4},{1,25},{... | collective-permute-start | bytes 491528 | tf_op jit(solution)/shard_map/ppermute | solution.py:62
  147.1 15.9 %collective-permute-start.56 = (bf16[64,1536]{1,0:T(8,128)(2,1)S(1)}, bf16[64,1536]{1,0:T(8,128)(2,1)S(1)}, u32[]{:S(2)}, u32[]{:S(2)}) collective-permute-start(bf16[64,1536]{1,0:T(8,128)(2,1)S(1)} %pad_maximum_fusion.10), channel_id=1, source_target_pairs={{0,3},{1,2},{2,1},{3,0},{4,7},{5,6},{6,5},{7,4},{8,11},{9,10},{10,... | collective-permute-start | bytes 589832 | tf_op jit(solution)/shard_map/ppermute | solution.py:62
  149.0 16.3 %collective-permute-start.55 = (bf16[64,1536]{1,0:T(8,128)(2,1)S(1)}, bf16[64,1536]{1,0:T(8,128)(2,1)S(1)}, u32[]{:S(2)}, u32[]{:S(2)}) collective-permute-start(bf16[64,1536]{1,0:T(8,128)(2,1)S(1)} %pad_maximum_fusion.10), channel_id=1, source_target_pairs={{0,2},{1,3},{2,0},{3,1},{4,6},{5,7},{6,4},{7,5},{8,10},{9,11},{10,... | collective-permute-start | bytes 589832 | tf_op jit(solution)/shard_map/ppermute | solution.py:62
  149.0 16.3 %collective-permute-start.54 = (bf16[64,1536]{1,0:T(8,128)(2,1)S(1)}, bf16[64,1536]{1,0:T(8,128)(2,1)S(1)}, u32[]{:S(2)}, u32[]{:S(2)}) collective-permute-start(bf16[64,1536]{1,0:T(8,128)(2,1)S(1)} %pad_maximum_fusion.10), channel_id=1, source_target_pairs={{0,1},{1,0},{2,3},{3,2},{4,5},{5,4},{6,7},{7,6},{8,9},{9,8},{10,11... | collective-permute-start | bytes 589832 | tf_op jit(solution)/shard_map/ppermute | solution.py:62
  181.6 15.4 %all-to-all-start = ((bf16[8,64,640]{2,1,0:T(8,128)(2,1)}), bf16[8,64,640]{2,1,0:T(8,128)(2,1)}, u32[]{:S(2)}, u32[]{:S(2)}) async-start(bf16[8,64,640]{2,1,0:T(8,128)(2,1)} %bitcast.405), calls=%async_computation | async-start | bytes 1310720 | tf_op jit(solution)/shard_map/all_to_all | solution.py:670
  185.8 237.7 %reduce-scatter.2.cloned.1.call-start = ((), (), s32[]{:S(2)}) async-start(), calls=%async_computation.5 | async-start | bytes 1310720 | tf_op jit(solution)/shard_map/reduce_scatter | solution.py:834
  219.7 16.4 %collective-permute-start.62 = (bf16[64,1024]{1,0:T(8,128)(2,1)}, bf16[64,1024]{1,0:T(8,128)(2,1)S(1)}, u32[]{:S(2)}, u32[]{:S(2)}) collective-permute-start(bf16[64,1024]{1,0:T(8,128)(2,1)} %get-tuple-element.323), channel_id=1, source_target_pairs={{0,3},{1,2},{2,1},{3,0},{4,7},{5,6},{6,5},{7,4},{8,11},{9,10},{10,... | collective-permute-start | bytes 393224 | tf_op jit(solution)/shard_map/ppermute | solution.py:62
  221.5 14.6 %collective-permute-start.61 = (bf16[64,1024]{1,0:T(8,128)(2,1)}, bf16[64,1024]{1,0:T(8,128)(2,1)}, u32[]{:S(2)}, u32[]{:S(2)}) collective-permute-start(bf16[64,1024]{1,0:T(8,128)(2,1)} %get-tuple-element.324), channel_id=1, source_target_pairs={{0,2},{1,3},{2,0},{3,1},{4,6},{5,7},{6,4},{7,5},{8,10},{9,11},{10,... | collective-permute-start | bytes 393224 | tf_op jit(solution)/shard_map/ppermute | solution.py:62
  221.5 15.3 %collective-permute-start.60 = (bf16[64,1024]{1,0:T(8,128)(2,1)}, bf16[64,1024]{1,0:T(8,128)(2,1)}, u32[]{:S(2)}, u32[]{:S(2)}) collective-permute-start(bf16[64,1024]{1,0:T(8,128)(2,1)} %get-tuple-element.325), channel_id=1, source_target_pairs={{0,1},{1,0},{2,3},{3,2},{4,5},{5,4},{6,7},{7,6},{8,9},{9,8},{10,11... | collective-permute-start | bytes 393224 | tf_op jit(solution)/shard_map/ppermute | solution.py:62
  241.2 15.4 %collective-permute-start.66 = (bf16[64,1536]{1,0:T(8,128)(2,1)S(1)}, bf16[64,1536]{1,0:T(8,128)(2,1)}, u32[]{:S(2)}, u32[]{:S(2)}) collective-permute-start(bf16[64,1536]{1,0:T(8,128)(2,1)S(1)} %pad_maximum_fusion.11), channel_id=1, source_target_pairs={{0,1},{1,0},{2,3},{3,2},{4,5},{5,4},{6,7},{7,6},{8,9},{9,8},{10,11... | collective-permute-start | bytes 589832 | tf_op jit(solution)/shard_map/ppermute | solution.py:62
  241.3 17.3 %collective-permute-start.67 = (bf16[64,1536]{1,0:T(8,128)(2,1)S(1)}, bf16[64,1536]{1,0:T(8,128)(2,1)}, u32[]{:S(2)}, u32[]{:S(2)}) collective-permute-start(bf16[64,1536]{1,0:T(8,128)(2,1)S(1)} %pad_maximum_fusion.11), channel_id=1, source_target_pairs={{0,2},{1,3},{2,0},{3,1},{4,6},{5,7},{6,4},{7,5},{8,10},{9,11},{10,... | collective-permute-start | bytes 589832 | tf_op jit(solution)/shard_map/ppermute | solution.py:62
  243.6 15.9 %collective-permute-start.68 = (bf16[64,1536]{1,0:T(8,128)(2,1)S(1)}, bf16[64,1536]{1,0:T(8,128)(2,1)}, u32[]{:S(2)}, u32[]{:S(2)}) collective-permute-start(bf16[64,1536]{1,0:T(8,128)(2,1)S(1)} %pad_maximum_fusion.11), channel_id=1, source_target_pairs={{0,3},{1,2},{2,1},{3,0},{4,7},{5,6},{6,5},{7,4},{8,11},{9,10},{10,... | collective-permute-start | bytes 589832 | tf_op jit(solution)/shard_map/ppermute | solution.py:62
  294.1 25.5 %collective-permute-start.70 = (bf16[256,512]{1,0:T(8,128)(2,1)S(1)}, bf16[256,512]{1,0:T(8,128)(2,1)S(1)}, u32[]{:S(2)}, u32[]{:S(2)}) collective-permute-start(bf16[256,512]{1,0:T(8,128)(2,1)S(1)} %copy-done.70), channel_id=1, source_target_pairs={{0,2},{1,3},{2,0},{3,1},{4,6},{5,7},{6,4},{7,5},{8,10},{9,11},{10,... | collective-permute-start | bytes 786440 | tf_op jit(solution)/shard_map/ppermute | solution.py:62
  296.5 23.1 %collective-permute-start.69 = (bf16[256,512]{1,0:T(8,128)(2,1)S(1)}, bf16[256,512]{1,0:T(8,128)(2,1)S(1)}, u32[]{:S(2)}, u32[]{:S(2)}) collective-permute-start(bf16[256,512]{1,0:T(8,128)(2,1)S(1)} %copy-done.69), channel_id=1, source_target_pairs={{0,1},{1,0},{2,3},{3,2},{4,5},{5,4},{6,7},{7,6},{8,9},{9,8},{10,11... | collective-permute-start | bytes 786440 | tf_op jit(solution)/shard_map/ppermute | solution.py:62
  297.5 22.2 %collective-permute-start.75 = (f32[8,2048]{1,0:T(8,128)S(1)}, f32[8,2048]{1,0:T(8,128)S(1)}, u32[]{:S(2)}, u32[]{:S(2)}) collective-permute-start(f32[8,2048]{1,0:T(8,128)S(1)} %copy-done.65), channel_id=1, source_target_pairs={{0,4},{4,0},{8,12},{12,8},{16,20},{20,16},{24,28},{28,24},{1,5},{5... | collective-permute-start | bytes 196616 | tf_op jit(solution)/shard_map/ppermute | solution.py:62
  302.1 28.2 %collective-permute-start.74 = (f32[8,4480]{1,0:T(8,128)S(1)}, f32[8,4480]{1,0:T(8,128)S(1)}, u32[]{:S(2)}, u32[]{:S(2)}) collective-permute-start(f32[8,4480]{1,0:T(8,128)S(1)} %add.662), channel_id=1, source_target_pairs={{0,16},{4,20},{8,24},{12,28},{16,0},{20,4},{24,8},{28,12},{1,17},{... | collective-permute-start | bytes 430088 | tf_op jit(solution)/shard_map/ppermute | solution.py:62
  325.9 20.6 %collective-permute-start.79 = (bf16[256,512]{1,0:T(8,128)(2,1)S(1)}, bf16[256,512]{1,0:T(8,128)(2,1)S(1)}, u32[]{:S(2)}, u32[]{:S(2)}) collective-permute-start(bf16[256,512]{1,0:T(8,128)(2,1)S(1)} %add_convert_fusion), channel_id=1, source_target_pairs={{0,2},{1,3},{2,0},{3,1},{4,6},{5,7},{6,4},{7,5},{8,10},{9,11},{10,... | collective-permute-start | bytes 786440 | tf_op jit(solution)/shard_map/ppermute | solution.py:62
  328.5 18.0 %collective-permute-start.80 = (bf16[256,512]{1,0:T(8,128)(2,1)S(1)}, bf16[256,512]{1,0:T(8,128)(2,1)S(1)}, u32[]{:S(2)}, u32[]{:S(2)}) collective-permute-start(bf16[256,512]{1,0:T(8,128)(2,1)S(1)} %add_convert_fusion), channel_id=1, source_target_pairs={{0,3},{1,2},{2,1},{3,0},{4,7},{5,6},{6,5},{7,4},{8,11},{9,10},{10,... | collective-permute-start | bytes 786440 | tf_op jit(solution)/shard_map/ppermute | solution.py:62
  347.7 82.9 %all-gather.12.cloned.1.call-start = ((), (), s32[]{:S(2)}) async-start(), calls=%async_computation.6 | async-start | bytes 2949120 | tf_op jit(solution)/shard_map/all_gather | solution.py:695
  350.2 137.2 %all-gather.14.cloned.1.call-start = ((), (), s32[]{:S(2)}) async-start(), calls=%async_computation.7 | async-start | bytes 1310720 | tf_op jit(solution)/shard_map/all_gather | solution.py:862
  374.0 24.8 %collective-permute-start.84 = (bf16[160,512]{1,0:T(8,128)(2,1)}, bf16[160,512]{1,0:T(8,128)(2,1)}, u32[]{:S(2)}, u32[]{:S(2)}) collective-permute-start(bf16[160,512]{1,0:T(8,128)(2,1)} %get-tuple-element.308), channel_id=1, source_target_pairs={{0,4},{4,0},{8,12},{12,8},{16,20},{20,16},{24,28},{28,24},{1,5},{5... | collective-permute-start | bytes 491528 | tf_op jit(solution)/shard_map/ppermute | solution.py:62
  374.0 26.9 %collective-permute-start.85 = (bf16[160,512]{1,0:T(8,128)(2,1)}, bf16[160,512]{1,0:T(8,128)(2,1)}, u32[]{:S(2)}, u32[]{:S(2)}) collective-permute-start(bf16[160,512]{1,0:T(8,128)(2,1)} %get-tuple-element.307), channel_id=1, source_target_pairs={{0,8},{4,12},{8,0},{12,4},{16,24},{20,28},{24,16},{28,20},{1,9},{5... | collective-permute-start | bytes 491528 | tf_op jit(solution)/shard_map/ppermute | solution.py:62
  378.5 24.5 %collective-permute-start.86 = (bf16[160,512]{1,0:T(8,128)(2,1)}, bf16[160,512]{1,0:T(8,128)(2,1)}, u32[]{:S(2)}, u32[]{:S(2)}) collective-permute-start(bf16[160,512]{1,0:T(8,128)(2,1)} %get-tuple-element.306), channel_id=1, source_target_pairs={{0,12},{4,8},{8,4},{12,0},{16,28},{20,24},{24,20},{28,16},{1,13},{... | collective-permute-start | bytes 491528 | tf_op jit(solution)/shard_map/ppermute | solution.py:62
  378.5 26.3 %collective-permute-start.87 = (bf16[160,512]{1,0:T(8,128)(2,1)}, bf16[160,512]{1,0:T(8,128)(2,1)}, u32[]{:S(2)}, u32[]{:S(2)}) collective-permute-start(bf16[160,512]{1,0:T(8,128)(2,1)} %get-tuple-element.305), channel_id=1, source_target_pairs={{0,16},{4,20},{8,24},{12,28},{16,0},{20,4},{24,8},{28,12},{1,17},{... | collective-permute-start | bytes 491528 | tf_op jit(solution)/shard_map/ppermute | solution.py:62
  401.9 18.3 %collective-permute-start.90 = (bf16[160,512]{1,0:T(8,128)(2,1)S(1)}, bf16[160,512]{1,0:T(8,128)(2,1)S(1)}, u32[]{:S(2)}, u32[]{:S(2)}) collective-permute-start(bf16[160,512]{1,0:T(8,128)(2,1)S(1)} %copy-done.75), channel_id=1, source_target_pairs={{0,28},{4,24},{8,20},{12,16},{16,12},{20,8},{24,4},{28,0},{1,29},{... | collective-permute-start | bytes 491528 | tf_op jit(solution)/shard_map/ppermute | solution.py:62
  424.1 51.8 %collective-permute-start.95 = (f32[8,1024]{1,0:T(8,128)S(1)}, f32[8,1024]{1,0:T(8,128)S(1)}, u32[]{:S(2)}, u32[]{:S(2)}) collective-permute-start(f32[8,1024]{1,0:T(8,128)S(1)} %get-tuple-element.202), channel_id=1, source_target_pairs={{0,2},{1,3},{2,0},{3,1},{4,6},{5,7},{6,4},{7,5},{8,10},{9,11},{10,... | collective-permute-start | bytes 98312 | tf_op jit(solution)/shard_map/ppermute | solution.py:62
  427.5 48.4 %collective-permute-start.96 = (f32[8,1024]{1,0:T(8,128)S(1)}, f32[8,1024]{1,0:T(8,128)S(1)}, u32[]{:S(2)}, u32[]{:S(2)}) collective-permute-start(f32[8,1024]{1,0:T(8,128)S(1)} %get-tuple-element.202), channel_id=1, source_target_pairs={{0,3},{1,2},{2,1},{3,0},{4,7},{5,6},{6,5},{7,4},{8,11},{9,10},{10,... | collective-permute-start | bytes 98312 | tf_op jit(solution)/shard_map/ppermute | solution.py:62
  429.3 46.7 %collective-permute-start.94 = (f32[8,1024]{1,0:T(8,128)S(1)}, f32[8,1024]{1,0:T(8,128)S(1)}, u32[]{:S(2)}, u32[]{:S(2)}) collective-permute-start(f32[8,1024]{1,0:T(8,128)S(1)} %get-tuple-element.202), channel_id=1, source_target_pairs={{0,1},{1,0},{2,3},{3,2},{4,5},{5,4},{6,7},{7,6},{8,9},{9,8},{10,11... | collective-permute-start | bytes 98312 | tf_op jit(solution)/shard_map/ppermute | solution.py:62
  (158 other events, 1437.8 us)
Sparse Core Ops, SparseCore 0:
  10.7 32.9 all-gather.5
  46.1 40.6 all-gather.7
  89.2 32.8 all-gather.9
  347.8 31.5 reduce-scatter.1
  381.9 37.0 all-gather.11
  430.6 27.0 all-gather.13
